TPU v7x, 256 devices: a whole 4x4x8 slice. The times are simulated.
256 devices in a mesh: seq: 32 (over y, x, core), head: 8 (over z).
Axes of the slice: x: 4, y: 4, z: 8, core: 2. Of those that a mesh axis runs over, the one named last changes fastest.
Arguments:
- q_values: bfloat16 [65536, 4096], P('seq', 'head'), may hold values from -6 to 6
- k_values: bfloat16 [65536, 4096], P('seq', 'head'), may hold values from -6 to 6
- v_values: bfloat16 [65536, 4096], P('seq', 'head'), may hold values from -6 to 6
- q_scales: float32 [65536, 32], P('seq', 'head'), may hold values from 0.5 to 4
- k_scales: float32 [65536, 32], P('seq', 'head'), may hold values from 0.5 to 4
- v_scales: float32 [65536, 32], P('seq', 'head'), may hold values from 0.5 to 2
- conv_weight: float32 [32, 33], P('head'), may hold values from -0.9 to 0.9
Outputs:
- attended: bfloat16 [65536, 4096], P('seq', 'head')
All inputs are finite; a program needn't handle non-finite values.
Results may differ from a plain program's by a relative error of at most 0.03.
Values may be sent and summed in bfloat16 or wider, within the bound.
A program may use at most 128 MiB of HBM per device.

v0:
```python
import functools

import jax
import jax.numpy as jnp
from jax import lax
from jax.sharding import Mesh
from jax.sharding import PartitionSpec as P

HEAD_DIM = 128
LANDMARKS = 256
SWEEPS = 6
SEQ = ("seq_0", "seq_1", "seq_2")


def side_by_side(arrays, axis, dim, along):
    both = jnp.concatenate(arrays, axis=along)
    result, at, finished = (lax.all_gather(both, axis, axis=dim, tiled=True), 0, [])
    for a in arrays:
        finished.append(lax.slice_in_dim(result, at, at + a.shape[along], axis=along))
        at += a.shape[along]
    return tuple(finished)


def from_everyone(shard, axis):
    copies = jnp.broadcast_to(shard, (lax.axis_size(axis), *shard.shape))
    return lax.all_to_all(copies, axis, split_axis=0, concat_axis=0, tiled=True)


def taken_together(shard, axis):
    everything = from_everyone(shard, axis)
    return jnp.max(everything, axis=0)


def packed_total(arrays, axis):
    line, at, finished = (jnp.concatenate([a.reshape(-1) for a in arrays]), 0, [])
    total = taken_together(line, axis)
    for a in arrays:
        finished.append(total[at : at + a.size].reshape(a.shape))
        at += a.size
    return tuple(finished)


def by_axis(shard, axes):
    return functools.reduce(lax.pmax, axes, shard)


def padded_2(shard, sides, width):
    for axis, dim in sides:
        count, length = (lax.axis_size(axis), shard.shape[dim])
        up = [(i, (i + 1) % count) for i in range(count - 1)]
        down = [(j, i) for i, j in up]
        last = lax.slice_in_dim(shard, length - width, length, axis=dim)
        leading = lax.slice_in_dim(shard, 0, width, axis=dim)
        before = lax.ppermute(last, axis, up)
        after = lax.ppermute(leading, axis, down)
        shard = jnp.concatenate([before, shard, after], axis=dim)
    return shard


def dequant(value_rows, scales):
    count = scales.shape[1]
    shaped = value_rows.reshape(value_rows.shape[0], count, HEAD_DIM).astype(jnp.float32)
    return (shaped * scales[:, :, None]).astype(jnp.bfloat16)


def newton(kernel, initial, right_side):
    eye_matrix = jnp.eye(kernel.shape[0], dtype=jnp.float32)
    iterate = initial
    for sweep in range(SWEEPS):
        product = jnp.dot(kernel, iterate)
        inner_term = 7.0 * eye_matrix - product
        inner_term = 15.0 * eye_matrix - jnp.dot(product, inner_term)
        inner_term = 13.0 * eye_matrix - jnp.dot(product, inner_term)
        iterate = 0.25 * jnp.dot(iterate, inner_term)
    return jnp.dot(iterate, right_side).astype(jnp.bfloat16)


def shards(q_values, k_values, v_values, q_scales, k_scales, v_scales, conv_weight):
    tok_rows = q_values.shape[0]
    head_count = q_scales.shape[1]
    seq_count = lax.axis_size(SEQ)
    marks_here = LANDMARKS // seq_count
    segment = tok_rows // marks_here
    query_rows = dequant(q_values, q_scales)
    key_rows = dequant(k_values, k_scales)
    value_rows = dequant(v_values, v_scales)

    def means(source):
        shaped = source.reshape(marks_here, segment, head_count, HEAD_DIM).astype(jnp.float32)
        return (
            jnp.mean(shaped, axis=1).astype(jnp.bfloat16).reshape(marks_here, head_count * HEAD_DIM)
        )

    query_landmarks, key_landmarks = side_by_side((means(query_rows), means(key_rows)), SEQ, 0, 1)
    query_landmarks = query_landmarks.reshape(LANDMARKS, head_count, HEAD_DIM)
    key_landmarks = key_landmarks.reshape(LANDMARKS, head_count, HEAD_DIM)
    pseudo_inverse_factor = HEAD_DIM ** (-0.5)
    landmark_kernel = (
        jnp.einsum(
            "jvc,kvc->vjk", query_landmarks, key_landmarks, preferred_element_type=jnp.float32
        )
        * pseudo_inverse_factor
    )
    middle = jax.nn.softmax(landmark_kernel, axis=-1)
    col_top = jnp.max(jnp.sum(middle, axis=1))
    row_top = jnp.max(jnp.sum(middle, axis=2))
    col_top, row_top = packed_total((col_top, row_top), "head")
    start = jnp.swapaxes(middle, 1, 2) / (col_top * row_top)
    distant_term = (
        jnp.einsum("kli,nli->lkn", query_landmarks, key_rows, preferred_element_type=jnp.float32)
        * pseudo_inverse_factor
    )
    far_top = by_axis(jnp.max(distant_term, axis=-1), SEQ)
    weight_matrix = jnp.exp(distant_term - far_top[:, :, None])
    total = jnp.sum(weight_matrix, axis=-1)
    summed = jnp.einsum(
        "lnx,xlj->nlj",
        weight_matrix.astype(jnp.bfloat16),
        value_rows,
        preferred_element_type=jnp.float32,
    )
    total, summed = (
        lax.psum(total.astype(jnp.bfloat16), SEQ).astype(jnp.float32),
        lax.psum(summed.astype(jnp.bfloat16), SEQ).astype(jnp.float32),
    )
    reduced = summed / jnp.swapaxes(total, 0, 1)[:, :, None]
    projected_values = jax.vmap(newton, in_axes=(0, 0, 1), out_axes=1)(middle, start, reduced)
    near_scores = (
        jnp.einsum("zea,uea->ezu", query_rows, key_landmarks, preferred_element_type=jnp.float32)
        * pseudo_inverse_factor
    )
    local_term = jax.nn.softmax(near_scores, axis=-1).astype(jnp.bfloat16)
    attended = jnp.einsum(
        "kbv,vkg->bkg", local_term, projected_values, preferred_element_type=jnp.float32
    ).reshape(tok_rows, head_count * HEAD_DIM)
    flat_values = value_rows.reshape(tok_rows, head_count * HEAD_DIM)
    tap_count = conv_weight.shape[1]
    padded = padded_2(flat_values, ((SEQ, 0),), tap_count // 2)
    tap_table = jnp.repeat(conv_weight, HEAD_DIM, axis=0)
    mixed = jnp.zeros((tok_rows, head_count * HEAD_DIM), jnp.float32)
    for tap_index in range(tap_count):
        mixed = (
            mixed
            + padded[tap_index : tap_index + tok_rows].astype(jnp.float32) * tap_table[:, tap_index]
        )
    return (attended + mixed).astype(jnp.bfloat16)


def solution(mesh):
    finer = Mesh(
        mesh.devices.reshape(4, 4, 2, mesh.shape["head"]), ("seq_0", "seq_1", "seq_2", "head")
    )
    placed = (
        P(SEQ, "head"),
        P(SEQ, "head"),
        P(SEQ, "head"),
        P(SEQ, "head"),
        P(SEQ, "head"),
        P(SEQ, "head"),
        P("head", None),
    )
    return jax.shard_map(
        shards, mesh=finer, in_specs=placed, out_specs=P(SEQ, "head"), check_vma=False
    )
```

profile of v0, /device:TPU:1, one launch (start us, length us, event | category | flops | bytes accessed | tf_op | source)
XLA Modules:
  0.0 301.6 jit_solution(4559212239840184039)
XLA Ops:
  6.5 4.7 %reshape.126 = f32[8,256,4,128]{3,2,1,0:T(4,128)} reshape(bf16[2048,512]{1,0:T(8,128)(2,1)} %param.7) | data formatting | bytes 6291456 | tf_op jit(solution)/shard_map/convert_element_type | solution.py:62
  11.7 4.6 %convert_reduce_fusion.1 = f32[8,4,128]{2,1,0:T(4,128)S(1)} fusion(f32[8,256,4,128]{3,2,1,0:T(4,128)} %reshape.126, f32[8,256,4]{2,1,0:T(8,128)S(1)} %bitcast.119), kind=kLoop, calls=%fused_computation.52 | loop fusion | flops 4190208 | bytes 4243456 | tf_op jit(solution)/shard_map/reduce_sum | solution.py:91
  16.3 3.0 %reshape.127 = f32[8,256,4,128]{3,2,1,0:T(4,128)} reshape(bf16[2048,512]{1,0:T(8,128)(2,1)S(1)} %copy-done.4) | data formatting | bytes 6291456 | tf_op jit(solution)/shard_map/convert_element_type | solution.py:62
  19.6 4.4 %convert_reduce_fusion = f32[8,4,128]{2,1,0:T(4,128)S(1)} fusion(f32[8,256,4,128]{3,2,1,0:T(4,128)} %reshape.127, f32[8,256,4]{2,1,0:T(8,128)S(1)} %bitcast.120), kind=kLoop, calls=%fused_computation.50 | loop fusion | flops 4190208 | bytes 4243456 | tf_op jit(solution)/shard_map/reduce_sum | solution.py:91
  24.1 26.4 %all_gather.3 = bf16[256,1024]{1,0:T(8,128)(2,1)S(1)} all-gather(bf16[8,1024]{1,0:T(8,128)(2,1)S(1)} %pad_maximum_fusion.2), channel_id=1, replica_groups=mesh['seq_0'=4,'seq_1'=4,'seq_2'=2,'head'=8] {'seq_0','seq_1','seq_2'}, dimensions={0}, use_global_device_ids=true | all-gather | bytes 540672 | tf_op jit(solution)/shard_map/all_gather | solution.py:17
  57.1 8.2 %all-to-all-start = ((f32[8,1,2]{2,1,0:T(1,128)}), f32[8,1,2]{2,1,0:T(1,128)S(1)}, u32[]{:S(2)}, u32[]{:S(2)}) async-start(f32[8,1,2]{2,1,0:T(1,128)} %broadcast_in_dim.4), calls=%async_computation | async-start | bytes 8192 | tf_op jit(solution)/shard_map/all_to_all | solution.py:26
  65.3 4.4 %multiply_reduce_fusion = (f32[4,256]{1,0:T(4,128)S(1)}, f32[4,256,2048]{2,1,0:T(8,128)}) fusion(bf16[256,4,128]{0,2,1:T(8,128)(2,1)S(1)} %bitcast.123, f32[2048,4]{0,1:T(4,128)S(1)} %copy-done.11, bf16[2048,512]{1,0:T(8,128)(2,1)S(1)} %copy-done.4), kind=kOutput, calls=%fused_computation.34 | convolution fusion | flops 544209920 | bytes 10784768 | tf_op jit(solution)/shard_map/kli,nli->lkn/dot_general | solution.py:110
  69.7 8.2 %pmax.21 = f32[4,256]{1,0:T(4,128)S(1)} all-reduce(f32[4,256]{1,0:T(4,128)S(1)} %get-tuple-element.48), channel_id=1, replica_groups=mesh['seq_0'=4,'seq_1'=4,'seq_2'=2,'head'=8] {'seq_0'}, use_global_device_ids=true, to_apply=%region_10.0 | all-reduce | flops 1024 | bytes 8192 | tf_op jit(solution)/shard_map/pmax | solution.py:44
  77.9 6.5 %pmax.22 = f32[4,256]{1,0:T(4,128)S(1)} all-reduce(f32[4,256]{1,0:T(4,128)S(1)} %pmax.21), channel_id=1, replica_groups=mesh['seq_0'=4,'seq_1'=4,'seq_2'=2,'head'=8] {'seq_1'}, use_global_device_ids=true, to_apply=%region_11.0 | all-reduce | flops 1024 | bytes 8192 | tf_op jit(solution)/shard_map/pmax | solution.py:44
  84.5 6.6 %pmax.23 = f32[4,256]{1,0:T(4,128)S(1)} all-reduce(f32[4,256]{1,0:T(4,128)S(1)} %pmax.22), channel_id=1, replica_groups=mesh['seq_0'=4,'seq_1'=4,'seq_2'=2,'head'=8] {'seq_2'}, use_global_device_ids=true, to_apply=%region_12.0 | all-reduce | flops 1024 | bytes 8192 | tf_op jit(solution)/shard_map/pmax | solution.py:44
  91.1 4.1 %copy.106 = f32[2048,512]{0,1:T(8,128)} copy(bf16[2048,512]{1,0:T(8,128)(2,1)} %param.9) | data formatting | bytes 6291456 | tf_op jit(solution)/shard_map/convert_element_type | solution.py:62
  95.2 2.7 multiply_convert_fusion.1
  97.9 5.9 %fusion.121 = bf16[256,4,128]{0,2,1:T(8,128)(2,1)} fusion(bf16[2048,4,128]{0,2,1:T(8,128)(2,1)S(1)} %multiply_convert_fusion.1, f32[4,256,2048]{2,1,0:T(8,128)} %get-tuple-element.49, f32[4,256]{1,0:T(4,128)S(1)} %pmax.23), kind=kOutput, calls=%fused_computation.148 | convolution fusion | flops 543293440 | bytes 10752000 | tf_op jit(solution)/shard_map/lnx,xlj->nlj/dot_general | solution.py:116
  104.0 3.1 %collective-permute-start = (bf16[16,512]{1,0:T(8,128)(2,1)S(1)}, bf16[16,512]{1,0:T(8,128)(2,1)S(1)}, u32[]{:S(2)}, u32[]{:S(2)}) collective-permute-start(bf16[16,512]{1,0:T(8,128)(2,1)S(1)} %copy.107), channel_id=1, source_target_pairs={{0,8},{8,16},{16,24},{24,32},{32,40},{40,48},{48,56},{56,64},{64,7... | collective-permute-start | bytes 49160 | tf_op jit(solution)/shard_map/ppermute | solution.py:54
  109.3 4.5 %fusion.2 = bf16[4,256]{1,0:T(4,128)(2,1)S(1)} fusion(f32[4,256,2048]{2,1,0:T(8,128)} %get-tuple-element.49, f32[4,256]{1,0:T(4,128)S(1)} %pmax.23), kind=kLoop, calls=%fused_computation.37 | loop fusion | flops 6290432 | bytes 8394752 | tf_op jit(solution)/shard_map/reduce_sum | solution.py:115
  113.8 4.2 %fusion.16 = f32[4,2048,256]{1,2,0:T(8,128)} fusion(bf16[256,4,128]{0,2,1:T(8,128)(2,1)S(1)} %bitcast.125, f32[2048,4]{0,1:T(4,128)S(1)} %copy-done.12, bf16[2048,512]{1,0:T(8,128)(2,1)S(1)} %copy-done.5), kind=kOutput, calls=%fused_computation.56 | convolution fusion | flops 540016640 | bytes 10780672 | tf_op jit(solution)/shard_map/zea,uea->ezu/dot_general | solution.py:129
  119.6 11.7 %fusion.170 = (f32[4,2048]{1,0:T(4,128)S(1)}, f32[4,2048,256]{1,2,0:T(8,128)}) fusion(f32[4,2048,256]{1,2,0:T(8,128)} %fusion.16), kind=kOutput, calls=%fused_computation.199 | output fusion | flops 8388863 | bytes 16809984 | tf_op jit(solution)/shard_map/sub | solution.py:132
  133.8 5.3 %copy.108 = f32[2048,512]{1,0:T(8,128)} copy(f32[2048,512]{0,1:T(8,128)} %bitcast.118) | data formatting | bytes 8388608 | tf_op jit(solution)/shard_map/mul | solution.py:63
  139.2 4.9 %multiply_convert_fusion = bf16[2048,512]{1,0:T(8,128)(2,1)} fusion(f32[2048,512]{1,0:T(8,128)} %copy.108, bf16[2048,512]{1,0:T(8,128)(2,1)} %param.9), kind=kLoop, calls=%fused_computation.45 | loop fusion | flops 3145728 | bytes 8388608 | tf_op jit(solution)/shard_map/convert_element_type | solution.py:63
  144.1 61.1 %psum.15 = bf16[256,4]{0,1:T(4,128)(2,1)S(1)} all-reduce(bf16[256,4]{0,1:T(4,128)(2,1)S(1)} %bitcast.164), channel_id=1, replica_groups=mesh['seq_0'=4,'seq_1'=4,'seq_2'=2,'head'=8] {'seq_0','seq_1','seq_2'}, use_global_device_ids=true, to_apply=%region_15.0 | all-reduce | flops 1024 | bytes 4096 | tf_op jit(solution)/shard_map/psum | solution.py:123
  210.9 4.3 %online-softmax = f32[4,256,256]{2,1,0:T(8,128)} custom-call(f32[4,256,256]{2,1,0:T(8,128)} %copy-done, f32[4,256,256]{2,1,0:T(8,128)} %convolution_multiply_fusion.5), custom_call_target="tpu_custom_call" | custom-call | tf_op online-softmax
  215.2 2.6 fusion.77
  219.2 4.3 %online-softmax.1 = f32[4,256,256]{2,1,0:T(8,128)} custom-call(f32[4,256,256]{2,1,0:T(8,128)} %copy-done, f32[4,256,256]{2,1,0:T(8,128)} %convolution_multiply_fusion.4), custom_call_target="tpu_custom_call" | custom-call | tf_op online-softmax
  223.5 2.6 fusion.86
  227.5 4.3 %online-softmax.2 = f32[4,256,256]{2,1,0:T(8,128)} custom-call(f32[4,256,256]{2,1,0:T(8,128)} %copy-done, f32[4,256,256]{2,1,0:T(8,128)} %convolution_multiply_fusion.3), custom_call_target="tpu_custom_call" | custom-call | tf_op online-softmax
  231.9 2.6 fusion.95
  235.8 4.3 %online-softmax.3 = f32[4,256,256]{2,1,0:T(8,128)} custom-call(f32[4,256,256]{2,1,0:T(8,128)} %copy-done, f32[4,256,256]{2,1,0:T(8,128)} %convolution_multiply_fusion.2), custom_call_target="tpu_custom_call" | custom-call | tf_op online-softmax
  240.2 2.6 fusion.104
  244.2 4.3 %online-softmax.4 = f32[4,256,256]{2,1,0:T(8,128)} custom-call(f32[4,256,256]{2,1,0:T(8,128)} %copy-done, f32[4,256,256]{2,1,0:T(8,128)} %convolution_multiply_fusion.1), custom_call_target="tpu_custom_call" | custom-call | tf_op online-softmax
  252.5 6.3 %fusion.13 = f32[4,128,2048]{2,1,0:T(8,128)} fusion(bf16[256,4,128]{2,0,1:T(8,128)(2,1)S(1)} %fusion.124, f32[4,2048,256]{1,2,0:T(8,128)} %get-tuple-element.51, f32[4,2048]{1,0:T(4,128)S(1)} %get-tuple-element.50), kind=kOutput, calls=%fused_computation.54 | convolution fusion | flops 541065216 | bytes 12877824 | tf_op jit(solution)/shard_map/kbv,vkg->bkg/dot_general | solution.py:133
  259.1 5.5 %copy.94 = f32[2048,512]{1,0:T(8,128)} copy(f32[2048,512]{0,1:T(8,128)} %bitcast.121) | data formatting | bytes 8388608 | tf_op jit(solution)/shard_map/reshape | solution.py:135
  264.9 29.8 %add_convert_fusion = bf16[2048,512]{1,0:T(8,128)(2,1)} fusion(f32[2048,512]{1,0:T(8,128)} %copy.94, bf16[2048,512]{1,0:T(8,128)(2,1)S(1)} %copy-done.6, bf16[16,512]{1,0:T(8,128)(2,1)S(1)} %collective-permute-done.1, bf16[16,512]{1,0:T(8,128)(2,1)S(1)} %collective-permute-done, f32[512]{0:T(512)S(1)} %bitcast.132, f32[512]{0:T(512)S(1)} %bitcast.133, ...), kind=kLoop, calls=%fused_computation.44 | loop fusion | flops 205520896 | bytes 8488960 | tf_op jit(solution)/shard_map/convert_element_type | solution.py:146
  (140 shorter events, 27.8 us)
Async XLA Ops:
  52.9 156.1 %copy-start = (f32[4,256,256]{2,1,0:T(8,128)}, f32[4,256,256]{2,1,0:T(8,128)S(1)}, u32[]{:S(2)}) copy-start(f32[4,256,256]{2,1,0:T(8,128)S(1)} %get-tuple-element.47) | copy-start | bytes 3145732
  57.1 148.1 %all-to-all-start = ((f32[8,1,2]{2,1,0:T(1,128)}), f32[8,1,2]{2,1,0:T(1,128)S(1)}, u32[]{:S(2)}, u32[]{:S(2)}) async-start(f32[8,1,2]{2,1,0:T(1,128)} %broadcast_in_dim.4), calls=%async_computation | async-start | bytes 8192 | tf_op jit(solution)/shard_map/all_to_all | solution.py:26
  65.3 185.8 %all-reduce.2.cloned.1.call-start = ((), (), s32[]{:S(2)}) async-start(), calls=%async_computation.1 | async-start | bytes 524288 | tf_op jit(solution)/shard_map/psum | solution.py:124
  69.7 25.5 %copy-start.10 = (f32[2048,4]{0,1:T(4,128)S(1)}, f32[2048,4]{0,1:T(4,128)}, u32[]{:S(2)}) copy-start(f32[2048,4]{0,1:T(4,128)} %param.12) | copy-start | bytes 98308
  104.0 160.6 %collective-permute-start = (bf16[16,512]{1,0:T(8,128)(2,1)S(1)}, bf16[16,512]{1,0:T(8,128)(2,1)S(1)}, u32[]{:S(2)}, u32[]{:S(2)}) collective-permute-start(bf16[16,512]{1,0:T(8,128)(2,1)S(1)} %copy.107), channel_id=1, source_target_pairs={{0,8},{8,16},{16,24},{24,32},{32,40},{40,48},{48,56},{56,64},{64,7... | collective-permute-start | bytes 49160 | tf_op jit(solution)/shard_map/ppermute | solution.py:54
  107.1 157.5 %collective-permute-start.1 = (bf16[16,512]{1,0:T(8,128)(2,1)S(1)}, bf16[16,512]{1,0:T(8,128)(2,1)S(1)}, u32[]{:S(2)}, u32[]{:S(2)}) collective-permute-start(bf16[16,512]{1,0:T(8,128)(2,1)S(1)} %copy.109), channel_id=1, source_target_pairs={{8,0},{16,8},{24,16},{32,24},{40,32},{48,40},{56,48},{64,56},{72,6... | collective-permute-start | bytes 49160 | tf_op jit(solution)/shard_map/ppermute | solution.py:55
  210.9 6.9 %copy-start.8 = (f32[4,256,256]{2,1,0:T(8,128)S(1)}, f32[4,256,256]{2,1,0:T(8,128)}, u32[]{:S(2)}) copy-start(f32[4,256,256]{2,1,0:T(8,128)} %convolution_multiply_fusion.5) | copy-start | bytes 3145732
  219.2 6.9 %copy-start.1 = (f32[4,256,256]{2,1,0:T(8,128)S(1)}, f32[4,256,256]{2,1,0:T(8,128)}, u32[]{:S(2)}) copy-start(f32[4,256,256]{2,1,0:T(8,128)} %convolution_multiply_fusion.4) | copy-start | bytes 3145732
  227.5 6.9 %copy-start.2 = (f32[4,256,256]{2,1,0:T(8,128)S(1)}, f32[4,256,256]{2,1,0:T(8,128)}, u32[]{:S(2)}) copy-start(f32[4,256,256]{2,1,0:T(8,128)} %convolution_multiply_fusion.3) | copy-start | bytes 3145732
  235.8 6.9 %copy-start.3 = (f32[4,256,256]{2,1,0:T(8,128)S(1)}, f32[4,256,256]{2,1,0:T(8,128)}, u32[]{:S(2)}) copy-start(f32[4,256,256]{2,1,0:T(8,128)} %convolution_multiply_fusion.2) | copy-start | bytes 3145732
  244.2 7.0 %copy-start.7 = (f32[4,256,256]{2,1,0:T(8,128)S(1)}, f32[4,256,256]{2,1,0:T(8,128)}, u32[]{:S(2)}) copy-start(f32[4,256,256]{2,1,0:T(8,128)} %convolution_multiply_fusion.1) | copy-start | bytes 3145732
  258.8 5.9 %copy-start.16 = (f32[512,1]{0,1:T(1,128)S(1)}, f32[512,1]{0,1:T(1,128)}, u32[]{:S(2)}) copy-start(f32[512,1]{0,1:T(1,128)} %get-tuple-element.15) | copy-start | bytes 6148
  258.8 5.9 %copy-start.17 = (f32[512,1]{0,1:T(1,128)S(1)}, f32[512,1]{0,1:T(1,128)}, u32[]{:S(2)}) copy-start(f32[512,1]{0,1:T(1,128)} %get-tuple-element.16) | copy-start | bytes 6148
  258.8 5.9 %copy-start.18 = (f32[512,1]{0,1:T(1,128)S(1)}, f32[512,1]{0,1:T(1,128)}, u32[]{:S(2)}) copy-start(f32[512,1]{0,1:T(1,128)} %get-tuple-element.17) | copy-start | bytes 6148
  258.8 5.9 %copy-start.19 = (f32[512,1]{0,1:T(1,128)S(1)}, f32[512,1]{0,1:T(1,128)}, u32[]{:S(2)}) copy-start(f32[512,1]{0,1:T(1,128)} %get-tuple-element.18) | copy-start | bytes 6148
  258.8 5.9 %copy-start.20 = (f32[512,1]{0,1:T(1,128)S(1)}, f32[512,1]{0,1:T(1,128)}, u32[]{:S(2)}) copy-start(f32[512,1]{0,1:T(1,128)} %get-tuple-element.19) | copy-start | bytes 6148
  258.8 5.9 %copy-start.21 = (f32[512,1]{0,1:T(1,128)S(1)}, f32[512,1]{0,1:T(1,128)}, u32[]{:S(2)}) copy-start(f32[512,1]{0,1:T(1,128)} %get-tuple-element.20) | copy-start | bytes 6148
  258.9 5.9 %copy-start.22 = (f32[512,1]{0,1:T(1,128)S(1)}, f32[512,1]{0,1:T(1,128)}, u32[]{:S(2)}) copy-start(f32[512,1]{0,1:T(1,128)} %get-tuple-element.21) | copy-start | bytes 6148
  258.9 5.9 %copy-start.23 = (f32[512,1]{0,1:T(1,128)S(1)}, f32[512,1]{0,1:T(1,128)}, u32[]{:S(2)}) copy-start(f32[512,1]{0,1:T(1,128)} %get-tuple-element.22) | copy-start | bytes 6148
  258.9 5.9 %copy-start.24 = (f32[512,1]{0,1:T(1,128)S(1)}, f32[512,1]{0,1:T(1,128)}, u32[]{:S(2)}) copy-start(f32[512,1]{0,1:T(1,128)} %get-tuple-element.23) | copy-start | bytes 6148
  258.9 5.9 %copy-start.25 = (f32[512,1]{0,1:T(1,128)S(1)}, f32[512,1]{0,1:T(1,128)}, u32[]{:S(2)}) copy-start(f32[512,1]{0,1:T(1,128)} %get-tuple-element.24) | copy-start | bytes 6148
  258.9 5.9 %copy-start.26 = (f32[512,1]{0,1:T(1,128)S(1)}, f32[512,1]{0,1:T(1,128)}, u32[]{:S(2)}) copy-start(f32[512,1]{0,1:T(1,128)} %get-tuple-element.25) | copy-start | bytes 6148
  258.9 5.9 %copy-start.27 = (f32[512,1]{0,1:T(1,128)S(1)}, f32[512,1]{0,1:T(1,128)}, u32[]{:S(2)}) copy-start(f32[512,1]{0,1:T(1,128)} %get-tuple-element.26) | copy-start | bytes 6148
  258.9 5.9 %copy-start.28 = (f32[512,1]{0,1:T(1,128)S(1)}, f32[512,1]{0,1:T(1,128)}, u32[]{:S(2)}) copy-start(f32[512,1]{0,1:T(1,128)} %get-tuple-element.27) | copy-start | bytes 6148
  258.9 5.9 %copy-start.29 = (f32[512,1]{0,1:T(1,128)S(1)}, f32[512,1]{0,1:T(1,128)}, u32[]{:S(2)}) copy-start(f32[512,1]{0,1:T(1,128)} %get-tuple-element.28) | copy-start | bytes 6148
  258.9 5.9 %copy-start.30 = (f32[512,1]{0,1:T(1,128)S(1)}, f32[512,1]{0,1:T(1,128)}, u32[]{:S(2)}) copy-start(f32[512,1]{0,1:T(1,128)} %get-tuple-element.29) | copy-start | bytes 6148
  258.9 5.9 %copy-start.31 = (f32[512,1]{0,1:T(1,128)S(1)}, f32[512,1]{0,1:T(1,128)}, u32[]{:S(2)}) copy-start(f32[512,1]{0,1:T(1,128)} %get-tuple-element.30) | copy-start | bytes 6148
  259.0 5.9 %copy-start.32 = (f32[512,1]{0,1:T(1,128)S(1)}, f32[512,1]{0,1:T(1,128)}, u32[]{:S(2)}) copy-start(f32[512,1]{0,1:T(1,128)} %get-tuple-element.31) | copy-start | bytes 6148
  259.0 5.9 %copy-start.33 = (f32[512,1]{0,1:T(1,128)S(1)}, f32[512,1]{0,1:T(1,128)}, u32[]{:S(2)}) copy-start(f32[512,1]{0,1:T(1,128)} %get-tuple-element.32) | copy-start | bytes 6148
  259.0 5.9 %copy-start.34 = (f32[512,1]{0,1:T(1,128)S(1)}, f32[512,1]{0,1:T(1,128)}, u32[]{:S(2)}) copy-start(f32[512,1]{0,1:T(1,128)} %get-tuple-element.33) | copy-start | bytes 6148
  259.0 5.9 %copy-start.35 = (f32[512,1]{0,1:T(1,128)S(1)}, f32[512,1]{0,1:T(1,128)}, u32[]{:S(2)}) copy-start(f32[512,1]{0,1:T(1,128)} %get-tuple-element.34) | copy-start | bytes 6148
  259.0 5.9 %copy-start.36 = (f32[512,1]{0,1:T(1,128)S(1)}, f32[512,1]{0,1:T(1,128)}, u32[]{:S(2)}) copy-start(f32[512,1]{0,1:T(1,128)} %get-tuple-element.35) | copy-start | bytes 6148
  (18 other events, 96.2 us)
Sparse Core Ops, SparseCore 0:
  103.9 108.5 all-reduce.1
where the time goes:
time: 304 us; the launch traced here: 302 us
  blocking collectives  109 us (36%)
  other arithmetic  66.2 us (22%)
  matrix products  45.7 us (15%)
  local copies, waits for them, and re-layouts  30.2 us (10%)
  Pallas kernels  21.7 us (7%)
  between operations  15.6 us (5%)
  starting transfers between devices  13.4 us (4%)
    psum x1, blocking collectives, shards(): lax.psum(total.astype(jnp.bfloat16), SEQ).astype(jnp.float32)  61.1 us
    convert_element_type x1, other arithmetic, shards(): return (attended + mixed).astype(jnp.bfloat16)  29.8 us
    all_gather x1, blocking collectives, side_by_side(): lax.all_gather(both, axis, axis=dim, tiled=True)  26.4 us
    unnamed x5, Pallas kernels  21.7 us
    pmax x3, blocking collectives, by_axis(): return functools.reduce(lax.pmax, axes, shard)  21.4 us
    dot_general x6, matrix products, newton(): inner_term = 13.0 * eye_matrix - jnp.dot(product, inner_term)  13.4 us
    convert_element_type x3, local copies, waits for them, and re-layouts, dequant(): value_rows.reshape(value_rows.shape[0], count, HEAD_DIM).astype(jnp.float32)  11.9 us
    sub x1, other arithmetic, shards(): local_term = jax.nn.softmax(near_scores, axis=-1).astype(jnp.bfloat16)  11.7 us
  transfers between devices with their start and end apart: 4, of which 0 were waited for; matrix products, arithmetic and copies ran while one was open for 29% of the time, Pallas kernels for 7%

commit v1 on v0

v1 whole, which is shorter than its diff:
```python
import functools
import math

import jax
import jax.numpy as jnp
from jax import lax
from jax.experimental import pallas as pl
from jax.experimental.pallas import tpu as pltpu
from jax.sharding import PartitionSpec as P

MESH = pl.DeviceIdType.MESH
F32 = jnp.float32
BF16 = jnp.bfloat16
HEAD_DIM = 128
LANDMARKS = 256
SWEEPS = 6
TAPS = 33
REACH = TAPS // 2
LOG2E = math.log2(math.e)
SCALE2 = HEAD_DIM**-0.5 * LOG2E
FACTOR = HEAD_DIM**-0.5

TOK = 2048
HEADS = 4
WIDTH = HEADS * HEAD_DIM
SEQN = 32
HEADN = 8
SEGS = 8
SEG = 256
OWN = 8
SLICE = HEAD_DIM // OWN
PACK = LANDMARKS + 128
NEAR_EARLY = 2


def dot(a, b):
    return jnp.dot(a, b, preferred_element_type=F32)


def dot_nt(a, b):
    return lax.dot_general(a, b, (((1,), (1,)), ((), ())), preferred_element_type=F32)


def cols(h):
    return slice(h * HEAD_DIM, (h + 1) * HEAD_DIM)


def kernel(
    q_hbm, k_hbm, v_hbm, qs_ref, ks_ref, vs_ref, cw_ref, out_hbm,
    q_v, k_v, v_raw, v_pad, vt, sc_qk, sc_v, lm_all, qm, km,
    mid, tops, score, wt, rs_send, rs_recv, x_ref, near, conv, mp_all, out_v, wpad, toep,
    q_sem, k_sem, v_sem, out_sem, lm_s, lm_r, halo_s, halo_r, top_s, top_r, rs_s, rs_r, mp_s, mp_r,
):
    me = lax.axis_index("seq")
    zme = lax.axis_index("head")
    yme, xme, cme = me // 8, (me // 2) % 4, me % 2
    h_me = 2 * ((xme + yme) % 2) + cme
    j_me = (me // 2) // 2
    b_me = h_me * OWN + j_me

    def partner(r):
        return (
            ((yme + r // 8) % 4) * 8 + ((xme + (r // 2) % 4) % 4) * 2 + (cme + r % 2) % 2
        )

    def owner(h, j):
        y = j // 2
        return (4 * y + 2 * (j % 2) + (h // 2 + y) % 2) * 2 + h % 2

    def rows_copy(src, dst, sem, i):
        rows = pl.ds(i * SEG, SEG)
        return pltpu.make_async_copy(src.at[rows], dst.at[rows], sem.at[i])

    for i in range(SEGS):
        rows_copy(q_hbm, q_v, q_sem, i).start()
        rows_copy(k_hbm, k_v, k_sem, i).start()
    for i in range(SEGS):
        rows_copy(v_hbm, v_raw, v_sem, i).start()

    barrier = pltpu.get_barrier_semaphore()

    def greet_seq(r, _):
        pl.semaphore_signal(barrier, inc=1, device_id=(partner(r), zme), device_id_type=MESH)
        return 0

    def greet_head(r, _):
        pl.semaphore_signal(
            barrier, inc=1, device_id=(me, (zme + r) % HEADN), device_id_type=MESH
        )
        return 0

    lax.fori_loop(1, SEQN, greet_seq, 0)
    lax.fori_loop(1, HEADN, greet_head, 0)

    sc_qk[...] = jnp.concatenate([qs_ref[...], ks_ref[...]], axis=0).T
    sc_v[...] = jnp.concatenate([vs_ref[...], vs_ref[...]], axis=0).T

    seg_id = lax.broadcasted_iota(jnp.int32, (SEGS, HEAD_DIM), 0)

    def scale_qk(i, marks):
        rows = pl.ds(pl.multiple_of(i * SEG, SEG), SEG)
        rows_copy(q_hbm, q_v, q_sem, i).wait()
        rows_copy(k_hbm, k_v, k_sem, i).wait()
        following = []
        for n in range(2 * HEADS):
            buf, h = (q_v, n) if n < HEADS else (k_v, n - HEADS)
            x = (buf[rows, cols(h)].astype(F32) * sc_qk[rows, n : n + 1]).astype(BF16)
            buf[rows, cols(h)] = x
            mean = jnp.sum(x.astype(F32), axis=0, keepdims=True) * (1.0 / SEG)
            following.append(jnp.where(seg_id == i, mean, marks[n]))
        return tuple(following)

    marks = lax.fori_loop(
        0, SEGS, scale_qk, (jnp.zeros((SEGS, HEAD_DIM), F32),) * (2 * HEADS)
    )
    for h in range(HEADS):
        both = jnp.concatenate([marks[h], marks[HEADS + h]], axis=0)
        lm_all[me, :, cols(h)] = both.astype(BF16)

    pl.semaphore_wait(barrier, SEQN - 1 + HEADN - 1)

    def lm_copy(r, slot):
        return pltpu.make_async_remote_copy(
            src_ref=lm_all.at[slot],
            dst_ref=lm_all.at[slot],
            send_sem=lm_s.at[r],
            recv_sem=lm_r.at[slot],
            device_id=(partner(r), zme),
            device_id_type=MESH,
        )

    def send_lm(r, _):
        lm_copy(r, me).start()
        return 0

    lax.fori_loop(1, SEQN, send_lm, 0)

    def scale_v(i, _):
        rows = pl.ds(pl.multiple_of(i * SEG, SEG), SEG)
        out_rows = pl.ds(pl.multiple_of(i * SEG + REACH, REACH), SEG)
        rows_copy(v_hbm, v_raw, v_sem, i).wait()
        for h in range(HEADS):
            x = (v_raw[rows, cols(h)].astype(F32) * sc_v[rows, h : h + 1]).astype(BF16)
            v_pad[out_rows, cols(h)] = x
            vt[h, :, rows] = x.astype(F32).T.astype(BF16)
        return 0

    lax.fori_loop(0, SEGS, scale_v, 0)
    v_pad[TOK + 2 * REACH :, :] = jnp.zeros((128 - 2 * REACH, WIDTH), BF16)

    after, before = (me + 1) % SEQN, (me + SEQN - 1) % SEQN
    down = pltpu.make_async_remote_copy(
        src_ref=v_pad.at[pl.ds(TOK, REACH)],
        dst_ref=v_pad.at[pl.ds(0, REACH)],
        send_sem=halo_s.at[0],
        recv_sem=halo_r.at[0],
        device_id=(after, zme),
        device_id_type=MESH,
    )
    up = pltpu.make_async_remote_copy(
        src_ref=v_pad.at[pl.ds(REACH, REACH)],
        dst_ref=v_pad.at[pl.ds(TOK + REACH, REACH)],
        send_sem=halo_s.at[1],
        recv_sem=halo_r.at[1],
        device_id=(before, zme),
        device_id_type=MESH,
    )
    down.start()
    up.start()

    wpad[...] = jnp.zeros_like(wpad)
    wpad[0:HEADS, 0:TAPS] = cw_ref[...]
    for h in range(HEADS):
        line = jnp.broadcast_to(wpad[h : h + 1, :], (128, 256))
        toep[h] = pltpu.roll(line, 0, 1, stride=1, stride_axis=0).astype(BF16)

    def conv_block(b):
        window = pl.ds(pl.multiple_of(b * 128, 128), 256)
        rows = pl.ds(pl.multiple_of(b * 128, 128), 128)
        for h in range(HEADS):
            conv[rows, cols(h)] = dot(toep[h], v_pad[window, cols(h)])

    def conv_inner(b, _):
        conv_block(b)
        return 0

    lax.fori_loop(1, TOK // 128 - 1, conv_inner, 0)

    def recv_lm(r, _):
        lm_copy(r, partner(r)).wait_recv()
        return 0

    lax.fori_loop(1, SEQN, recv_lm, 0)
    for h in range(HEADS):
        both = lm_all[:, :, cols(h)].astype(F32)
        qm[h] = both[:, :SEGS].reshape(LANDMARKS, HEAD_DIM).astype(BF16)
        km[h] = both[:, SEGS:].reshape(LANDMARKS, HEAD_DIM).astype(BF16)

    col_top = jnp.zeros((1, 1), F32)
    row_top = jnp.zeros((1, 1), F32)
    for h in range(HEADS):
        s = dot_nt(qm[h], km[h])
        e = jnp.exp2((s - jnp.max(s, axis=1, keepdims=True)) * SCALE2)
        m = e / jnp.sum(e, axis=1, keepdims=True)
        mid[h] = m
        c = jnp.sum(m, axis=0, keepdims=True)
        r = jnp.sum(m, axis=1, keepdims=True)
        col_top = jnp.maximum(col_top, jnp.max(c, axis=1, keepdims=True))
        row_top = jnp.maximum(row_top, jnp.max(r, axis=0, keepdims=True))
    first_half = lax.broadcasted_iota(jnp.int32, (8, 128), 0) < 4
    tops[zme] = jnp.where(
        first_half, jnp.broadcast_to(col_top, (8, 128)), jnp.broadcast_to(row_top, (8, 128))
    )

    def top_copy(r, slot):
        return pltpu.make_async_remote_copy(
            src_ref=tops.at[slot],
            dst_ref=tops.at[slot],
            send_sem=top_s.at[r],
            recv_sem=top_r.at[slot],
            device_id=(me, (zme + r) % HEADN),
            device_id_type=MESH,
        )

    def send_top(r, _):
        top_copy(r, zme).start()
        return 0

    lax.fori_loop(1, HEADN, send_top, 0)

    def rs_copy(block, slot, target):
        return pltpu.make_async_remote_copy(
            src_ref=rs_send.at[block],
            dst_ref=rs_recv.at[slot],
            send_sem=rs_s.at[block],
            recv_sem=rs_r.at[slot],
            device_id=(target, zme),
            device_id_type=MESH,
        )

    row_id = lax.broadcasted_iota(jnp.int32, (SLICE, 128), 0)
    for h in range(HEADS):
        def far_scores(i, top):
            rows = pl.ds(pl.multiple_of(i * SEG, SEG), SEG)
            s = dot_nt(k_v[rows, cols(h)], qm[h])
            score[rows, :] = s
            return jnp.maximum(top, jnp.max(s.reshape(SEG // 8, 8, LANDMARKS), axis=0))

        top = lax.fori_loop(0, SEGS, far_scores, jnp.full((8, LANDMARKS), -jnp.inf, F32))
        top = jnp.max(top, axis=0, keepdims=True).astype(BF16).astype(F32)

        def far_weights(i, total):
            rows = pl.ds(pl.multiple_of(i * SEG, SEG), SEG)
            e = jnp.exp2((score[rows, :] - top) * SCALE2)
            wt[rows, :] = e.astype(BF16)
            return total + jnp.sum(e.reshape(SEG // 8, 8, LANDMARKS), axis=0)

        total = lax.fori_loop(0, SEGS, far_weights, jnp.zeros((8, LANDMARKS), F32))
        total = jnp.sum(total, axis=0, keepdims=True)
        total_hi = total.astype(BF16).astype(F32)
        total_lo = total - total_hi
        summed = dot(vt[h], wt[...])
        facts = jnp.zeros((SLICE, 128), F32)
        for n, (vec, half) in enumerate(
            (v, half) for v in (top, total_hi, total_lo) for half in range(2)
        ):
            part = jnp.broadcast_to(vec[:, half * 128 : (half + 1) * 128], (SLICE, 128))
            facts = jnp.where(row_id == n, part, facts)
        rs_send[h * OWN : (h + 1) * OWN, :, 0:LANDMARKS] = (
            summed.astype(BF16).reshape(OWN, SLICE, LANDMARKS)
        )
        rs_send[h * OWN : (h + 1) * OWN, :, LANDMARKS:PACK] = jnp.broadcast_to(
            facts.astype(BF16)[None], (OWN, SLICE, 128)
        )

        def send_rs(n, _):
            j = (n + j_me) % OWN
            target = owner(h, j)
            block = h * OWN + j

            @pl.when(target != me)
            def _():
                rs_copy(block, me, target).start()

            return 0

        lax.fori_loop(0, OWN, send_rs, 0)
    rs_recv[me] = rs_send[b_me]

    down.wait_recv()
    up.wait_recv()
    v_pad[0:REACH, :] = jnp.where(me == 0, jnp.zeros((REACH, WIDTH), BF16), v_pad[0:REACH, :])
    v_pad[TOK + REACH : TOK + 2 * REACH, :] = jnp.where(
        me == SEQN - 1, jnp.zeros((REACH, WIDTH), BF16), v_pad[TOK + REACH : TOK + 2 * REACH, :]
    )
    conv_block(0)
    conv_block(TOK // 128 - 1)

    def recv_top(r, _):
        top_copy(r, (zme + r) % HEADN).wait_recv()
        return 0

    lax.fori_loop(1, HEADN, recv_top, 0)
    best = jnp.max(tops[...], axis=0)
    scale = 1.0 / (best[0:1, 0:1] * best[4:5, 0:1])
    m = mid[h_me]
    mb = m.astype(BF16)
    x_ref[0:LANDMARKS, :] = dot(m.T.astype(BF16), mb) * scale
    x_ref[LANDMARKS:, :] = m * scale

    def sweep(_, carry):
        x = x_ref[...]
        xb = x.astype(BF16)
        y = dot(xb, xb[:LANDMARKS])
        b = (7.0 * x[:LANDMARKS] - y[:LANDMARKS]).astype(BF16)
        x_ref[...] = 0.25 * (13.0 * x - 15.0 * y + dot(y.astype(BF16), b))
        return carry

    lax.fori_loop(0, SWEEPS, sweep, 0)

    def near_softmax(h):
        def chunk(i, _):
            rows = pl.ds(pl.multiple_of(i * 128, 128), 128)
            s = dot_nt(q_v[rows, cols(h)], km[h])
            e = jnp.exp2((s - jnp.max(s, axis=1, keepdims=True)) * SCALE2)
            near[h, rows, :] = (e * (1.0 / jnp.sum(e, axis=1, keepdims=True))).astype(BF16)
            return 0

        lax.fori_loop(0, TOK // 128, chunk, 0)

    for h in range(NEAR_EARLY):
        near_softmax(h)

    def recv_rs(r, _):
        rs_copy(0, partner(r), me).wait_recv()
        return 0

    lax.fori_loop(1, SEQN, recv_rs, 0)

    def facts_top(s, top):
        return jnp.maximum(top, rs_recv[s, :, LANDMARKS:PACK].astype(F32))

    top = lax.fori_loop(0, SEQN, facts_top, jnp.full((SLICE, 128), -jnp.inf, F32))

    def combine(s, carry):
        num, den = carry
        facts = rs_recv[s, :, LANDMARKS:PACK].astype(F32)
        e = jnp.exp2((facts - top) * SCALE2)
        w = jnp.concatenate([e[0:1], e[1:2]], axis=1)
        part = jnp.concatenate([facts[2:3] + facts[4:5], facts[3:4] + facts[5:6]], axis=1)
        return num + rs_recv[s, :, 0:LANDMARKS].astype(F32) * w, den + part * w

    num, den = lax.fori_loop(
        0, SEQN, combine, (jnp.zeros((SLICE, LANDMARKS), F32), jnp.zeros((1, LANDMARKS), F32))
    )
    reduced = (num / den).astype(BF16)
    mp_all[b_me] = dot(reduced, x_ref[LANDMARKS:, :].astype(BF16)).astype(BF16)

    def mp_copy(r, slot):
        return pltpu.make_async_remote_copy(
            src_ref=mp_all.at[slot],
            dst_ref=mp_all.at[slot],
            send_sem=mp_s.at[r],
            recv_sem=mp_r.at[slot],
            device_id=(partner(r), zme),
            device_id_type=MESH,
        )

    def send_mp(r, _):
        mp_copy(r, b_me).start()
        return 0

    lax.fori_loop(1, SEQN, send_mp, 0)

    for h in range(NEAR_EARLY, HEADS):
        near_softmax(h)

    for h in range(HEADS):
        for j in range(OWN):
            b = h * OWN + j

            @pl.when(b != b_me)
            def _():
                mp_copy(0, b).wait_recv()

    mapped = [
        mp_all[h * OWN : (h + 1) * OWN].reshape(HEAD_DIM, LANDMARKS).astype(F32).T.astype(BF16)
        for h in range(HEADS)
    ]
    step = 512
    for i in range(TOK // step):
        rows = slice(i * step, (i + 1) * step)
        for h in range(HEADS):
            out_v[rows, cols(h)] = (dot(near[h, rows, :], mapped[h]) + conv[rows, cols(h)]).astype(
                BF16
            )
        pltpu.make_async_copy(out_v.at[rows], out_hbm.at[rows], out_sem.at[i]).start()

    down.wait_send()
    up.wait_send()

    def sent(r, _):
        lm_copy(r, me).wait_send()
        mp_copy(r, b_me).wait_send()
        return 0

    lax.fori_loop(1, SEQN, sent, 0)

    def sent_top(r, _):
        top_copy(r, zme).wait_send()
        return 0

    lax.fori_loop(1, HEADN, sent_top, 0)

    def sent_rs(b, _):
        @pl.when(b != b_me)
        def _():
            rs_copy(b, me, me).wait_send()

        return 0

    lax.fori_loop(0, SEQN, sent_rs, 0)
    for i in range(TOK // step):
        rows = slice(i * step, (i + 1) * step)
        pltpu.make_async_copy(out_v.at[rows], out_hbm.at[rows], out_sem.at[i]).wait()


def shards(q, k, v, qs, ks, vs, cw):
    dma = pltpu.SemaphoreType.DMA
    vm = pltpu.VMEM
    whole = pl.BlockSpec(memory_space=pltpu.VMEM)
    hbm = pl.BlockSpec(memory_space=pl.ANY)
    return pl.pallas_call(
        kernel,
        out_shape=jax.ShapeDtypeStruct((TOK, WIDTH), BF16),
        in_specs=[hbm, hbm, hbm, whole, whole, whole, whole],
        out_specs=hbm,
        scratch_shapes=[
            vm((TOK, WIDTH), BF16),
            vm((TOK, WIDTH), BF16),
            vm((TOK, WIDTH), BF16),
            vm((TOK + 128, WIDTH), BF16),
            vm((HEADS, HEAD_DIM, TOK), BF16),
            vm((TOK, 8), F32),
            vm((TOK, 8), F32),
            vm((SEQN, 2 * SEGS, WIDTH), BF16),
            vm((HEADS, LANDMARKS, HEAD_DIM), BF16),
            vm((HEADS, LANDMARKS, HEAD_DIM), BF16),
            vm((HEADS, LANDMARKS, LANDMARKS), F32),
            vm((HEADN, 8, 128), F32),
            vm((TOK, LANDMARKS), F32),
            vm((TOK, LANDMARKS), BF16),
            vm((SEQN, SLICE, PACK), BF16),
            vm((SEQN, SLICE, PACK), BF16),
            vm((2 * LANDMARKS, LANDMARKS), F32),
            vm((HEADS, TOK, LANDMARKS), BF16),
            vm((TOK, WIDTH), F32),
            vm((SEQN, SLICE, LANDMARKS), BF16),
            vm((TOK, WIDTH), BF16),
            vm((8, 256), F32),
            vm((HEADS, 128, 256), BF16),
            dma((SEGS,)),
            dma((SEGS,)),
            dma((SEGS,)),
            dma((4,)),
            dma((SEQN,)),
            dma((SEQN,)),
            dma((2,)),
            dma((2,)),
            dma((HEADN,)),
            dma((HEADN,)),
            dma((SEQN,)),
            dma((SEQN,)),
            dma((SEQN,)),
            dma((SEQN,)),
        ],
        compiler_params=pltpu.CompilerParams(
            collective_id=0, has_side_effects=True, vmem_limit_bytes=48 * 1024 * 1024
        ),
        name="nystrom",
    )(q, k, v, qs.T, ks.T, vs.T, cw)


def solution(mesh):
    tokens, heads = P("seq", "head"), P("head", None)
    return jax.shard_map(
        shards, mesh=mesh, in_specs=(tokens,) * 6 + (heads,), out_specs=tokens, check_vma=False
    )
```

time: 304 us -> 70 us (0.23)
  blocking collectives: 109 us -> 0 us
  other arithmetic: 66.2 us -> 0 us
  matrix products: 45.7 us -> 0 us
  Pallas kernels: 21.7 us -> 63.8 us
  local copies, waits for them, and re-layouts: 30.2 us -> 5.87 us
  between operations: 15.6 us -> 0.01 us
  starting transfers between devices: 13.4 us -> 0 us
    pallas_call x0 -> x1, Pallas kernels: none -> 63.8 us  [shards(): pl.pallas_call(kernel, out_shape=jax.ShapeDtypeStruct((TOK, WIDTH), BF16)...]
    psum x1 -> x0, blocking collectives: 61.1 us -> none  [shards(): lax.psum(total.astype(jnp.bfloat16), SEQ).astype(jnp.float32)]
    dot_general x18 -> x0, matrix products: 45.7 us -> none  [the longest x6 13.4 us: newton(): inner_term = 13.0 * eye_matrix - jnp.dot(product, inner_term)]
    convert_element_type x3 -> x0, other arithmetic: 37.4 us -> none  [the longest x1 29.8 us: shards(): return (attended + mixed).astype(jnp.bfloat16)]
    all_gather x1 -> x0, blocking collectives: 26.4 us -> none  [side_by_side(): lax.all_gather(both, axis, axis=dim, tiled=True)]
    unnamed x5 -> x0, Pallas kernels: 21.7 us -> none
    pmax x3 -> x0, blocking collectives: 21.4 us -> none  [by_axis(): return functools.reduce(lax.pmax, axes, shard)]
    reduce_sum x5 -> x0, other arithmetic: 14.3 us -> none  [the longest x2 8.93 us: means(): jnp.mean(shaped, axis=1).astype(jnp.bfloat16)]
  transfers between devices with their start and end apart: 4 -> 0, of which waited for: 0 -> 0; matrix products, arithmetic and copies ran while one was open for 29% -> 0% of each run, Pallas kernels for 7% -> 0%
where the time goes in v1:
time: 70 us; the launch traced here: 69.6 us
  Pallas kernels  63.8 us (91%)
  local copies, waits for them, and re-layouts  5.87 us (8%)
    pallas_call x1, Pallas kernels, shards(): pl.pallas_call(kernel, out_shape=jax.ShapeDtypeStruct((TOK, WIDTH), BF16)...  63.8 us
    unnamed x11, local copies, waits for them, and re-layouts  5.87 us

profile of v1, /device:TPU:1, one launch (start us, length us, event | category | flops | bytes accessed | tf_op | source)
XLA Modules:
  0.0 69.6 jit_solution(8802290256362667534)
XLA Ops:
  0.0 0.0 copy-start
  0.0 1.6 %copy-done = bf16[2048,512]{1,0:T(8,128)(2,1)S(1)} copy-done((bf16[2048,512]{1,0:T(8,128)(2,1)S(1)}, bf16[2048,512]{1,0:T(8,128)(2,1)}, u32[]{:S(2)}) %copy-start) | copy-done | bytes 2097176
  1.6 0.0 copy-start.1
  1.6 0.8 %copy-done.1 = f32[2048,4]{0,1:T(4,128)S(1)} copy-done((f32[2048,4]{0,1:T(4,128)S(1)}, f32[2048,4]{0,1:T(4,128)}, u32[]{:S(2)}) %copy-start.1) | copy-done | bytes 32792
  2.4 0.0 copy-start.2
  2.4 0.8 %copy-done.2 = f32[2048,4]{0,1:T(4,128)S(1)} copy-done((f32[2048,4]{0,1:T(4,128)S(1)}, f32[2048,4]{0,1:T(4,128)}, u32[]{:S(2)}) %copy-start.2) | copy-done | bytes 32792
  3.1 0.0 copy-start.3
  3.1 0.8 %copy-done.3 = f32[2048,4]{0,1:T(4,128)S(1)} copy-done((f32[2048,4]{0,1:T(4,128)S(1)}, f32[2048,4]{0,1:T(4,128)}, u32[]{:S(2)}) %copy-start.3) | copy-done | bytes 32792
  3.9 0.0 copy-start.4
  3.9 0.7 copy-done.4
  4.5 63.8 %nystrom.1 = bf16[2048,512]{1,0:T(8,128)(2,1)S(1)} custom-call(bf16[2048,512]{1,0:T(8,128)(2,1)S(1)} %copy-done, bf16[2048,512]{1,0:T(8,128)(2,1)} %k_hbm.1, bf16[2048,512]{1,0:T(8,128)(2,1)} %v_hbm.1, f32[4,2048]{1,0:T(4,128)S(1)} %bitcast.3, f32[4,2048]{1,0:T(4,128)S(1)} %bitcast.4, f32[4,2048]{1,0:T(4,128)S(1)} %bitcast.5, f32[4,33]{1,0:T(4,128)S(1)} %copy-done.4), custom_call_target="tpu_custom_call" | custom-call | tf_op jit(solution)/shard_map/nystrom/pallas_call | solution.py:433
  68.3 1.3 %copy.9 = bf16[2048,512]{1,0:T(8,128)(2,1)} copy(bf16[2048,512]{1,0:T(8,128)(2,1)S(1)} %nystrom.1) | data formatting | bytes 4194304
Async XLA Ops:
  0.0 1.6 %copy-start = (bf16[2048,512]{1,0:T(8,128)(2,1)S(1)}, bf16[2048,512]{1,0:T(8,128)(2,1)}, u32[]{:S(2)}) copy-start(bf16[2048,512]{1,0:T(8,128)(2,1)} %q_hbm.1) | copy-start | bytes 6291460
  1.6 0.8 %copy-start.1 = (f32[2048,4]{0,1:T(4,128)S(1)}, f32[2048,4]{0,1:T(4,128)}, u32[]{:S(2)}) copy-start(f32[2048,4]{0,1:T(4,128)} %param.10) | copy-start | bytes 98308
  2.4 0.8 %copy-start.2 = (f32[2048,4]{0,1:T(4,128)S(1)}, f32[2048,4]{0,1:T(4,128)}, u32[]{:S(2)}) copy-start(f32[2048,4]{0,1:T(4,128)} %param.11) | copy-start | bytes 98308
  3.1 0.8 %copy-start.3 = (f32[2048,4]{0,1:T(4,128)S(1)}, f32[2048,4]{0,1:T(4,128)}, u32[]{:S(2)}) copy-start(f32[2048,4]{0,1:T(4,128)} %param.12) | copy-start | bytes 98308
  3.9 0.7 copy-start.4

commit v2 on v1

--- a/solution.py
+++ b/solution.py
@@ -30,7 +30,7 @@
 OWN = 8
 SLICE = HEAD_DIM // OWN
 PACK = LANDMARKS + 128
-NEAR_EARLY = 2
+NEAR_EARLY = 4
 
 
 def dot(a, b):
@@ -46,10 +46,10 @@
 
 
 def kernel(
-    q_hbm, k_hbm, v_hbm, qs_ref, ks_ref, vs_ref, cw_ref, out_hbm,
-    q_v, k_v, v_raw, v_pad, vt, sc_qk, sc_v, lm_all, qm, km,
+    q_hbm, k_hbm, v_hbm, qs_hbm, ks_hbm, vs_hbm, cw_hbm, out_hbm,
+    scales, taps, q_v, k_v, v_raw, v_pad, vt, sc_qk, sc_v, lm_all, qm, km, kmt,
     mid, tops, score, wt, rs_send, rs_recv, x_ref, near, conv, mp_all, out_v, wpad, toep,
-    q_sem, k_sem, v_sem, out_sem, lm_s, lm_r, halo_s, halo_r, top_s, top_r, rs_s, rs_r, mp_s, mp_r,
+    sc_sem, q_sem, k_sem, v_sem, out_sem, lm_s, lm_r, halo_s, halo_r, top_s, top_r, rs_s, rs_r, mp_s, mp_r,
 ):
     me = lax.axis_index("seq")
     zme = lax.axis_index("head")
@@ -71,6 +71,19 @@
         rows = pl.ds(i * SEG, SEG)
         return pltpu.make_async_copy(src.at[rows], dst.at[rows], sem.at[i])
 
+    small = [
+        pltpu.make_async_copy(src, dst, sc_sem.at[n])
+        for n, (src, dst) in enumerate(
+            (
+                (qs_hbm, scales.at[0]),
+                (ks_hbm, scales.at[1]),
+                (vs_hbm, scales.at[2]),
+                (cw_hbm, taps),
+            )
+        )
+    ]
+    for copy in small:
+        copy.start()
     for i in range(SEGS):
         rows_copy(q_hbm, q_v, q_sem, i).start()
         rows_copy(k_hbm, k_v, k_sem, i).start()
@@ -92,8 +105,10 @@
     lax.fori_loop(1, SEQN, greet_seq, 0)
     lax.fori_loop(1, HEADN, greet_head, 0)
 
-    sc_qk[...] = jnp.concatenate([qs_ref[...], ks_ref[...]], axis=0).T
-    sc_v[...] = jnp.concatenate([vs_ref[...], vs_ref[...]], axis=0).T
+    for copy in small:
+        copy.wait()
+    sc_qk[...] = jnp.concatenate([scales[0], scales[1]], axis=0).T
+    sc_v[...] = jnp.concatenate([scales[2], scales[2]], axis=0).T
 
     seg_id = lax.broadcasted_iota(jnp.int32, (SEGS, HEAD_DIM), 0)
 
@@ -119,6 +134,7 @@
 
     pl.semaphore_wait(barrier, SEQN - 1 + HEADN - 1)
 
+
     def lm_copy(r, slot):
         return pltpu.make_async_remote_copy(
             src_ref=lm_all.at[slot],
@@ -145,7 +161,7 @@
             vt[h, :, rows] = x.astype(F32).T.astype(BF16)
         return 0
 
-    lax.fori_loop(0, SEGS, scale_v, 0)
+    lax.fori_loop(0, SEGS, scale_v, 0, unroll=2)
     v_pad[TOK + 2 * REACH :, :] = jnp.zeros((128 - 2 * REACH, WIDTH), BF16)
 
     after, before = (me + 1) % SEQN, (me + SEQN - 1) % SEQN
@@ -169,7 +185,7 @@
     up.start()
 
     wpad[...] = jnp.zeros_like(wpad)
-    wpad[0:HEADS, 0:TAPS] = cw_ref[...]
+    wpad[0:HEADS, 0:TAPS] = taps[...]
     for h in range(HEADS):
         line = jnp.broadcast_to(wpad[h : h + 1, :], (128, 256))
         toep[h] = pltpu.roll(line, 0, 1, stride=1, stride_axis=0).astype(BF16)
@@ -184,7 +200,7 @@
         conv_block(b)
         return 0
 
-    lax.fori_loop(1, TOK // 128 - 1, conv_inner, 0)
+    lax.fori_loop(1, TOK // 128 - 1, conv_inner, 0, unroll=2)
 
     def recv_lm(r, _):
         lm_copy(r, partner(r)).wait_recv()
@@ -194,12 +210,14 @@
     for h in range(HEADS):
         both = lm_all[:, :, cols(h)].astype(F32)
         qm[h] = both[:, :SEGS].reshape(LANDMARKS, HEAD_DIM).astype(BF16)
-        km[h] = both[:, SEGS:].reshape(LANDMARKS, HEAD_DIM).astype(BF16)
+        keys = both[:, SEGS:].reshape(LANDMARKS, HEAD_DIM)
+        km[h] = keys.astype(BF16)
+        kmt[h] = keys.T.astype(BF16)
 
     col_top = jnp.zeros((1, 1), F32)
     row_top = jnp.zeros((1, 1), F32)
     for h in range(HEADS):
-        s = dot_nt(qm[h], km[h])
+        s = dot(qm[h], kmt[h])
         e = jnp.exp2((s - jnp.max(s, axis=1, keepdims=True)) * SCALE2)
         m = e / jnp.sum(e, axis=1, keepdims=True)
         mid[h] = m
@@ -246,7 +264,9 @@
             score[rows, :] = s
             return jnp.maximum(top, jnp.max(s.reshape(SEG // 8, 8, LANDMARKS), axis=0))
 
-        top = lax.fori_loop(0, SEGS, far_scores, jnp.full((8, LANDMARKS), -jnp.inf, F32))
+        top = lax.fori_loop(
+            0, SEGS, far_scores, jnp.full((8, LANDMARKS), -jnp.inf, F32), unroll=True
+        )
         top = jnp.max(top, axis=0, keepdims=True).astype(BF16).astype(F32)
 
         def far_weights(i, total):
@@ -255,7 +275,9 @@
             wt[rows, :] = e.astype(BF16)
             return total + jnp.sum(e.reshape(SEG // 8, 8, LANDMARKS), axis=0)
 
-        total = lax.fori_loop(0, SEGS, far_weights, jnp.zeros((8, LANDMARKS), F32))
+        total = lax.fori_loop(
+            0, SEGS, far_weights, jnp.zeros((8, LANDMARKS), F32), unroll=True
+        )
         total = jnp.sum(total, axis=0, keepdims=True)
         total_hi = total.astype(BF16).astype(F32)
         total_lo = total - total_hi
@@ -301,6 +323,7 @@
         return 0
 
     lax.fori_loop(1, HEADN, recv_top, 0)
+
     best = jnp.max(tops[...], axis=0)
     scale = 1.0 / (best[0:1, 0:1] * best[4:5, 0:1])
     m = mid[h_me]
@@ -318,24 +341,22 @@
 
     lax.fori_loop(0, SWEEPS, sweep, 0)
 
-    def near_softmax(h):
-        def chunk(i, _):
-            rows = pl.ds(pl.multiple_of(i * 128, 128), 128)
-            s = dot_nt(q_v[rows, cols(h)], km[h])
+    def near_softmax(i, _):
+        rows = pl.ds(pl.multiple_of(i * SEG, SEG), SEG)
+        for h in range(HEADS):
+            s = dot(q_v[rows, cols(h)], kmt[h])
             e = jnp.exp2((s - jnp.max(s, axis=1, keepdims=True)) * SCALE2)
             near[h, rows, :] = (e * (1.0 / jnp.sum(e, axis=1, keepdims=True))).astype(BF16)
-            return 0
-
-        lax.fori_loop(0, TOK // 128, chunk, 0)
-
-    for h in range(NEAR_EARLY):
-        near_softmax(h)
+        return 0
+
+    lax.fori_loop(0, NEAR_EARLY, near_softmax, 0)
 
     def recv_rs(r, _):
         rs_copy(0, partner(r), me).wait_recv()
         return 0
 
     lax.fori_loop(1, SEQN, recv_rs, 0)
+
 
     def facts_top(s, top):
         return jnp.maximum(top, rs_recv[s, :, LANDMARKS:PACK].astype(F32))
@@ -372,8 +393,8 @@
 
     lax.fori_loop(1, SEQN, send_mp, 0)
 
-    for h in range(NEAR_EARLY, HEADS):
-        near_softmax(h)
+    lax.fori_loop(NEAR_EARLY, SEGS, near_softmax, 0)
+
 
     for h in range(HEADS):
         for j in range(OWN):
@@ -428,14 +449,15 @@
 def shards(q, k, v, qs, ks, vs, cw):
     dma = pltpu.SemaphoreType.DMA
     vm = pltpu.VMEM
-    whole = pl.BlockSpec(memory_space=pltpu.VMEM)
     hbm = pl.BlockSpec(memory_space=pl.ANY)
     return pl.pallas_call(
         kernel,
         out_shape=jax.ShapeDtypeStruct((TOK, WIDTH), BF16),
-        in_specs=[hbm, hbm, hbm, whole, whole, whole, whole],
+        in_specs=[hbm] * 7,
         out_specs=hbm,
         scratch_shapes=[
+            vm((3, HEADS, TOK), F32),
+            vm((HEADS, TAPS), F32),
             vm((TOK, WIDTH), BF16),
             vm((TOK, WIDTH), BF16),
             vm((TOK, WIDTH), BF16),
@@ -446,6 +468,7 @@
             vm((SEQN, 2 * SEGS, WIDTH), BF16),
             vm((HEADS, LANDMARKS, HEAD_DIM), BF16),
             vm((HEADS, LANDMARKS, HEAD_DIM), BF16),
+            vm((HEADS, HEAD_DIM, LANDMARKS), BF16),
             vm((HEADS, LANDMARKS, LANDMARKS), F32),
             vm((HEADN, 8, 128), F32),
             vm((TOK, LANDMARKS), F32),
@@ -459,6 +482,7 @@
             vm((TOK, WIDTH), BF16),
             vm((8, 256), F32),
             vm((HEADS, 128, 256), BF16),
+            dma((4,)),
             dma((SEGS,)),
             dma((SEGS,)),
             dma((SEGS,)),
@@ -475,7 +499,7 @@
             dma((SEQN,)),
         ],
         compiler_params=pltpu.CompilerParams(
-            collective_id=0, has_side_effects=True, vmem_limit_bytes=48 * 1024 * 1024
+            collective_id=0, has_side_effects=True, vmem_limit_bytes=62 * 1024 * 1024
         ),
         name="nystrom",
     )(q, k, v, qs.T, ks.T, vs.T, cw)

time: 70 us -> 48.6 us (0.69)
  Pallas kernels: 63.8 us -> 45.4 us
  local copies, waits for them, and re-layouts: 5.87 us -> 3.05 us
    pallas_call x1, Pallas kernels: 63.8 us -> 45.4 us  [shards(): pl.pallas_call(kernel, out_shape=jax.ShapeDtypeStruct((TOK, WIDTH), BF16)...]
    unnamed x11 -> x1, local copies, waits for them, and re-layouts: 5.87 us -> 3.05 us
where the time goes in v2:
time: 48.6 us; the launch traced here: 48.5 us
  Pallas kernels  45.4 us (93%)
  local copies, waits for them, and re-layouts  3.05 us (6%)
    pallas_call x1, Pallas kernels, shards(): pl.pallas_call(kernel, out_shape=jax.ShapeDtypeStruct((TOK, WIDTH), BF16)...  45.4 us
    unnamed x1, local copies, waits for them, and re-layouts  3.05 us

profile of v2, /device:TPU:1, one launch (start us, length us, event | category | flops | bytes accessed | tf_op | source)
XLA Modules:
  0.0 48.5 jit_solution(6848893532541210111)
XLA Ops:
  0.0 45.4 %nystrom.1 = bf16[2048,512]{1,0:T(8,128)(2,1)} custom-call(bf16[2048,512]{1,0:T(8,128)(2,1)} %q_hbm.1, bf16[2048,512]{1,0:T(8,128)(2,1)} %k_hbm.1, bf16[2048,512]{1,0:T(8,128)(2,1)} %v_hbm.1, f32[4,2048]{1,0:T(4,128)} %bitcast.3, f32[4,2048]{1,0:T(4,128)} %bitcast.4, f32[4,2048]{1,0:T(4,128)} %bitcast.5, f32[4,33]{1,0:T(4,128)} %cw_hbm.1), custom_call_target="tpu_custom_call" | custom-call | tf_op jit(solution)/shard_map/nystrom/pallas_call | solution.py:453
  45.4 3.0 %copy.9 = bf16[2048,512]{1,0:T(8,128)(2,1)} copy(bf16[2048,512]{1,0:T(8,128)(2,1)} %nystrom.1) | data formatting | bytes 4194304

commit v3 on v2

--- a/solution.py
+++ b/solution.py
@@ -27,6 +27,7 @@
 HEADN = 8
 SEGS = 8
 SEG = 256
+CHIPS = SEQN // 2
 OWN = 8
 SLICE = HEAD_DIM // OWN
 PACK = LANDMARKS + 128
@@ -46,23 +47,27 @@
 
 
 def kernel(
-    q_hbm, k_hbm, v_hbm, qs_hbm, ks_hbm, vs_hbm, cw_hbm, out_hbm,
-    scales, taps, q_v, k_v, v_raw, v_pad, vt, sc_qk, sc_v, lm_all, qm, km, kmt,
-    mid, tops, score, wt, rs_send, rs_recv, x_ref, near, conv, mp_all, out_v, wpad, toep,
-    sc_sem, q_sem, k_sem, v_sem, out_sem, lm_s, lm_r, halo_s, halo_r, top_s, top_r, rs_s, rs_r, mp_s, mp_r,
+    q_hbm, k_hbm, v_hbm, small, out,
+    q_v, k_v, v_raw, v_pad, vt, sc_qk, sc_v, lm_all, qm, km, kmt,
+    mid, tops, score, wt, rs_send, rs_recv, x_ref, near, conv, mp_all, toep,
+    q_sem, k_sem, v_sem, lm_s, lm_r, halo_s, halo_r, top_s, top_r, rs_s, rs_r, mp_s, mp_r,
 ):
     me = lax.axis_index("seq")
     zme = lax.axis_index("head")
     yme, xme, cme = me // 8, (me // 2) % 4, me % 2
     h_me = 2 * ((xme + yme) % 2) + cme
     j_me = (me // 2) // 2
-    b_me = h_me * OWN + j_me
+    chip = me // 2
+    other = me + 1 - 2 * cme
 
     def partner(r):
         return (
             ((yme + r // 8) % 4) * 8 + ((xme + (r // 2) % 4) % 4) * 2 + (cme + r % 2) % 2
         )
 
+    def across(r):
+        return ((yme + r // 4) % 4) * 8 + ((xme + r % 4) % 4) * 2 + cme
+
     def owner(h, j):
         y = j // 2
         return (4 * y + 2 * (j % 2) + (h // 2 + y) % 2) * 2 + h % 2
@@ -71,24 +76,9 @@
         rows = pl.ds(i * SEG, SEG)
         return pltpu.make_async_copy(src.at[rows], dst.at[rows], sem.at[i])
 
-    small = [
-        pltpu.make_async_copy(src, dst, sc_sem.at[n])
-        for n, (src, dst) in enumerate(
-            (
-                (qs_hbm, scales.at[0]),
-                (ks_hbm, scales.at[1]),
-                (vs_hbm, scales.at[2]),
-                (cw_hbm, taps),
-            )
-        )
-    ]
-    for copy in small:
-        copy.start()
     for i in range(SEGS):
         rows_copy(q_hbm, q_v, q_sem, i).start()
         rows_copy(k_hbm, k_v, k_sem, i).start()
-    for i in range(SEGS):
-        rows_copy(v_hbm, v_raw, v_sem, i).start()
 
     barrier = pltpu.get_barrier_semaphore()
 
@@ -105,10 +95,8 @@
     lax.fori_loop(1, SEQN, greet_seq, 0)
     lax.fori_loop(1, HEADN, greet_head, 0)
 
-    for copy in small:
-        copy.wait()
-    sc_qk[...] = jnp.concatenate([scales[0], scales[1]], axis=0).T
-    sc_v[...] = jnp.concatenate([scales[2], scales[2]], axis=0).T
+    sc_qk[...] = small[0 : 2 * HEADS, :].T
+    sc_v[...] = small[2 * HEADS : 4 * HEADS, :].T
 
     seg_id = lax.broadcasted_iota(jnp.int32, (SEGS, HEAD_DIM), 0)
 
@@ -116,6 +104,7 @@
         rows = pl.ds(pl.multiple_of(i * SEG, SEG), SEG)
         rows_copy(q_hbm, q_v, q_sem, i).wait()
         rows_copy(k_hbm, k_v, k_sem, i).wait()
+        rows_copy(v_hbm, v_raw, v_sem, i).start()
         following = []
         for n in range(2 * HEADS):
             buf, h = (q_v, n) if n < HEADS else (k_v, n - HEADS)
@@ -130,26 +119,25 @@
     )
     for h in range(HEADS):
         both = jnp.concatenate([marks[h], marks[HEADS + h]], axis=0)
-        lm_all[me, :, cols(h)] = both.astype(BF16)
+        lm_all[cme, chip, :, cols(h)] = both.astype(BF16)
 
     pl.semaphore_wait(barrier, SEQN - 1 + HEADN - 1)
 
-
-    def lm_copy(r, slot):
+    def group_copy(buf, at, sems, n, target):
         return pltpu.make_async_remote_copy(
-            src_ref=lm_all.at[slot],
-            dst_ref=lm_all.at[slot],
-            send_sem=lm_s.at[r],
-            recv_sem=lm_r.at[slot],
-            device_id=(partner(r), zme),
+            src_ref=buf.at[at],
+            dst_ref=buf.at[at],
+            send_sem=sems[0].at[n],
+            recv_sem=sems[1].at[n],
+            device_id=(target, zme),
             device_id_type=MESH,
         )
 
-    def send_lm(r, _):
-        lm_copy(r, me).start()
-        return 0
-
-    lax.fori_loop(1, SEQN, send_lm, 0)
+    for r in range(1, CHIPS):
+        group_copy(lm_all, (cme, chip), (lm_s, lm_r), 0, across(r)).start()
+    lm_total = group_copy(lm_all, (0, pl.ds(0, CHIPS - 1)), (lm_s, lm_r), 0, other)
+    lm_out = group_copy(lm_all, (cme,), (lm_s, lm_r), 1, other)
+    lm_in = group_copy(lm_all, (1 - cme,), (lm_s, lm_r), 1, other)
 
     def scale_v(i, _):
         rows = pl.ds(pl.multiple_of(i * SEG, SEG), SEG)
@@ -184,10 +172,8 @@
     down.start()
     up.start()
 
-    wpad[...] = jnp.zeros_like(wpad)
-    wpad[0:HEADS, 0:TAPS] = taps[...]
-    for h in range(HEADS):
-        line = jnp.broadcast_to(wpad[h : h + 1, :], (128, 256))
+    for h in range(HEADS):
+        line = jnp.broadcast_to(small[3 * HEADS + h : 3 * HEADS + h + 1, 0:256], (128, 256))
         toep[h] = pltpu.roll(line, 0, 1, stride=1, stride_axis=0).astype(BF16)
 
     def conv_block(b):
@@ -202,13 +188,13 @@
 
     lax.fori_loop(1, TOK // 128 - 1, conv_inner, 0, unroll=2)
 
-    def recv_lm(r, _):
-        lm_copy(r, partner(r)).wait_recv()
-        return 0
-
-    lax.fori_loop(1, SEQN, recv_lm, 0)
-    for h in range(HEADS):
-        both = lm_all[:, :, cols(h)].astype(F32)
+    lm_total.wait_recv()
+    lm_out.start()
+
+    lm_in.wait_recv()
+
+    for h in range(HEADS):
+        both = lm_all[:, :, :, cols(h)].reshape(SEQN, 2 * SEGS, HEAD_DIM).astype(F32)
         qm[h] = both[:, :SEGS].reshape(LANDMARKS, HEAD_DIM).astype(BF16)
         keys = both[:, SEGS:].reshape(LANDMARKS, HEAD_DIM)
         km[h] = keys.astype(BF16)
@@ -230,28 +216,26 @@
         first_half, jnp.broadcast_to(col_top, (8, 128)), jnp.broadcast_to(row_top, (8, 128))
     )
 
-    def top_copy(r, slot):
+    def top_copy(at, target):
         return pltpu.make_async_remote_copy(
-            src_ref=tops.at[slot],
-            dst_ref=tops.at[slot],
-            send_sem=top_s.at[r],
-            recv_sem=top_r.at[slot],
-            device_id=(me, (zme + r) % HEADN),
+            src_ref=tops.at[at],
+            dst_ref=tops.at[at],
+            send_sem=top_s.at[0],
+            recv_sem=top_r.at[0],
+            device_id=(me, target),
             device_id_type=MESH,
         )
 
-    def send_top(r, _):
-        top_copy(r, zme).start()
-        return 0
-
-    lax.fori_loop(1, HEADN, send_top, 0)
+    for r in range(1, HEADN):
+        top_copy(zme, (zme + r) % HEADN).start()
+    top_total = top_copy(pl.ds(0, HEADN - 1), zme)
 
     def rs_copy(block, slot, target):
         return pltpu.make_async_remote_copy(
             src_ref=rs_send.at[block],
             dst_ref=rs_recv.at[slot],
-            send_sem=rs_s.at[block],
-            recv_sem=rs_r.at[slot],
+            send_sem=rs_s.at[0],
+            recv_sem=rs_r.at[0],
             device_id=(target, zme),
             device_id_type=MESH,
         )
@@ -295,19 +279,16 @@
             facts.astype(BF16)[None], (OWN, SLICE, 128)
         )
 
-        def send_rs(n, _):
+
+    for h in range(HEADS):
+        for n in range(1, OWN):
             j = (n + j_me) % OWN
-            target = owner(h, j)
-            block = h * OWN + j
-
-            @pl.when(target != me)
-            def _():
-                rs_copy(block, me, target).start()
-
-            return 0
-
-        lax.fori_loop(0, OWN, send_rs, 0)
-    rs_recv[me] = rs_send[b_me]
+            rs_copy(h * OWN + j, me, owner(h, j)).start()
+    for n in range(1, HEADS):
+        h = (h_me + n) % HEADS
+        rs_copy(h * OWN + j_me, me, owner(h, j_me)).start()
+    rs_total = rs_copy(pl.ds(0, SEQN - 1), pl.ds(0, SEQN - 1), other)
+    rs_recv[me] = rs_send[h_me * OWN + j_me]
 
     down.wait_recv()
     up.wait_recv()
@@ -318,11 +299,17 @@
     conv_block(0)
     conv_block(TOK // 128 - 1)
 
-    def recv_top(r, _):
-        top_copy(r, (zme + r) % HEADN).wait_recv()
+    def near_softmax(i, _):
+        rows = pl.ds(pl.multiple_of(i * SEG, SEG), SEG)
+        for h in range(HEADS):
+            s = dot(q_v[rows, cols(h)], kmt[h])
+            e = jnp.exp2((s - jnp.max(s, axis=1, keepdims=True)) * SCALE2)
+            near[h, rows, :] = (e * (1.0 / jnp.sum(e, axis=1, keepdims=True))).astype(BF16)
         return 0
 
-    lax.fori_loop(1, HEADN, recv_top, 0)
+    lax.fori_loop(0, NEAR_EARLY, near_softmax, 0)
+
+    top_total.wait_recv()
 
     best = jnp.max(tops[...], axis=0)
     scale = 1.0 / (best[0:1, 0:1] * best[4:5, 0:1])
@@ -341,21 +328,7 @@
 
     lax.fori_loop(0, SWEEPS, sweep, 0)
 
-    def near_softmax(i, _):
-        rows = pl.ds(pl.multiple_of(i * SEG, SEG), SEG)
-        for h in range(HEADS):
-            s = dot(q_v[rows, cols(h)], kmt[h])
-            e = jnp.exp2((s - jnp.max(s, axis=1, keepdims=True)) * SCALE2)
-            near[h, rows, :] = (e * (1.0 / jnp.sum(e, axis=1, keepdims=True))).astype(BF16)
-        return 0
-
-    lax.fori_loop(0, NEAR_EARLY, near_softmax, 0)
-
-    def recv_rs(r, _):
-        rs_copy(0, partner(r), me).wait_recv()
-        return 0
-
-    lax.fori_loop(1, SEQN, recv_rs, 0)
+    rs_total.wait_recv()
 
 
     def facts_top(s, top):
@@ -375,89 +348,57 @@
         0, SEQN, combine, (jnp.zeros((SLICE, LANDMARKS), F32), jnp.zeros((1, LANDMARKS), F32))
     )
     reduced = (num / den).astype(BF16)
-    mp_all[b_me] = dot(reduced, x_ref[LANDMARKS:, :].astype(BF16)).astype(BF16)
-
-    def mp_copy(r, slot):
-        return pltpu.make_async_remote_copy(
-            src_ref=mp_all.at[slot],
-            dst_ref=mp_all.at[slot],
-            send_sem=mp_s.at[r],
-            recv_sem=mp_r.at[slot],
-            device_id=(partner(r), zme),
-            device_id_type=MESH,
-        )
-
-    def send_mp(r, _):
-        mp_copy(r, b_me).start()
-        return 0
-
-    lax.fori_loop(1, SEQN, send_mp, 0)
+    slot = (h_me // 2) * OWN + j_me
+    mp_all[cme, slot] = dot(reduced, x_ref[LANDMARKS:, :].astype(BF16)).astype(BF16)
+    for r in range(1, CHIPS):
+        group_copy(mp_all, (cme, slot), (mp_s, mp_r), 0, across(r)).start()
+    mp_total = group_copy(mp_all, (0, pl.ds(0, CHIPS - 1)), (mp_s, mp_r), 0, other)
+    mp_out = group_copy(mp_all, (cme,), (mp_s, mp_r), 1, other)
+    mp_in = group_copy(mp_all, (1 - cme,), (mp_s, mp_r), 1, other)
 
     lax.fori_loop(NEAR_EARLY, SEGS, near_softmax, 0)
 
-
-    for h in range(HEADS):
-        for j in range(OWN):
-            b = h * OWN + j
-
-            @pl.when(b != b_me)
-            def _():
-                mp_copy(0, b).wait_recv()
-
-    mapped = [
-        mp_all[h * OWN : (h + 1) * OWN].reshape(HEAD_DIM, LANDMARKS).astype(F32).T.astype(BF16)
-        for h in range(HEADS)
-    ]
-    step = 512
-    for i in range(TOK // step):
-        rows = slice(i * step, (i + 1) * step)
-        for h in range(HEADS):
-            out_v[rows, cols(h)] = (dot(near[h, rows, :], mapped[h]) + conv[rows, cols(h)]).astype(
-                BF16
-            )
-        pltpu.make_async_copy(out_v.at[rows], out_hbm.at[rows], out_sem.at[i]).start()
+    mp_total.wait_recv()
+    mp_out.start()
+
+    def attend(h):
+        lanes = pl.ds(pl.multiple_of(h * HEAD_DIM, HEAD_DIM), HEAD_DIM)
+        mapped = mp_all[h % 2, pl.ds((h // 2) * OWN, OWN)].reshape(HEAD_DIM, LANDMARKS).astype(F32).T.astype(BF16)
+        for i in range(4):
+            rows = slice(i * 512, (i + 1) * 512)
+            out[rows, lanes] = (dot(near[h, rows, :], mapped) + conv[rows, lanes]).astype(BF16)
+
+    attend(cme)
+    attend(cme + 2)
+
+    mp_in.wait_recv()
+
+    attend(1 - cme)
+    attend(3 - cme)
 
     down.wait_send()
     up.wait_send()
-
-    def sent(r, _):
-        lm_copy(r, me).wait_send()
-        mp_copy(r, b_me).wait_send()
-        return 0
-
-    lax.fori_loop(1, SEQN, sent, 0)
-
-    def sent_top(r, _):
-        top_copy(r, zme).wait_send()
-        return 0
-
-    lax.fori_loop(1, HEADN, sent_top, 0)
-
-    def sent_rs(b, _):
-        @pl.when(b != b_me)
-        def _():
-            rs_copy(b, me, me).wait_send()
-
-        return 0
-
-    lax.fori_loop(0, SEQN, sent_rs, 0)
-    for i in range(TOK // step):
-        rows = slice(i * step, (i + 1) * step)
-        pltpu.make_async_copy(out_v.at[rows], out_hbm.at[rows], out_sem.at[i]).wait()
+    lm_total.wait_send()
+    lm_out.wait_send()
+    top_total.wait_send()
+    rs_total.wait_send()
+    mp_total.wait_send()
+    mp_out.wait_send()
 
 
 def shards(q, k, v, qs, ks, vs, cw):
     dma = pltpu.SemaphoreType.DMA
     vm = pltpu.VMEM
     hbm = pl.BlockSpec(memory_space=pl.ANY)
+    whole = pl.BlockSpec(memory_space=pltpu.VMEM)
+    taps = jnp.pad(cw, ((0, 0), (0, TOK - TAPS)))
+    small = jnp.concatenate([qs.T, ks.T, vs.T, taps], axis=0)
     return pl.pallas_call(
         kernel,
         out_shape=jax.ShapeDtypeStruct((TOK, WIDTH), BF16),
-        in_specs=[hbm] * 7,
-        out_specs=hbm,
+        in_specs=[hbm, hbm, hbm, whole],
+        out_specs=whole,
         scratch_shapes=[
-            vm((3, HEADS, TOK), F32),
-            vm((HEADS, TAPS), F32),
             vm((TOK, WIDTH), BF16),
             vm((TOK, WIDTH), BF16),
             vm((TOK, WIDTH), BF16),
@@ -465,7 +406,7 @@
             vm((HEADS, HEAD_DIM, TOK), BF16),
             vm((TOK, 8), F32),
             vm((TOK, 8), F32),
-            vm((SEQN, 2 * SEGS, WIDTH), BF16),
+            vm((2, CHIPS, 2 * SEGS, WIDTH), BF16),
             vm((HEADS, LANDMARKS, HEAD_DIM), BF16),
             vm((HEADS, LANDMARKS, HEAD_DIM), BF16),
             vm((HEADS, HEAD_DIM, LANDMARKS), BF16),
@@ -478,31 +419,27 @@
             vm((2 * LANDMARKS, LANDMARKS), F32),
             vm((HEADS, TOK, LANDMARKS), BF16),
             vm((TOK, WIDTH), F32),
-            vm((SEQN, SLICE, LANDMARKS), BF16),
-            vm((TOK, WIDTH), BF16),
-            vm((8, 256), F32),
+            vm((2, CHIPS, SLICE, LANDMARKS), BF16),
             vm((HEADS, 128, 256), BF16),
-            dma((4,)),
             dma((SEGS,)),
             dma((SEGS,)),
             dma((SEGS,)),
-            dma((4,)),
-            dma((SEQN,)),
-            dma((SEQN,)),
-            dma((2,)),
-            dma((2,)),
-            dma((HEADN,)),
-            dma((HEADN,)),
-            dma((SEQN,)),
-            dma((SEQN,)),
-            dma((SEQN,)),
-            dma((SEQN,)),
+            dma((2,)),
+            dma((2,)),
+            dma((2,)),
+            dma((2,)),
+            dma((1,)),
+            dma((1,)),
+            dma((1,)),
+            dma((1,)),
+            dma((2,)),
+            dma((2,)),
         ],
         compiler_params=pltpu.CompilerParams(
-            collective_id=0, has_side_effects=True, vmem_limit_bytes=62 * 1024 * 1024
+            collective_id=0, has_side_effects=True, vmem_limit_bytes=50 * 1024 * 1024
         ),
         name="nystrom",
-    )(q, k, v, qs.T, ks.T, vs.T, cw)
+    )(q, k, v, small)
 
 
 def solution(mesh):

time: 48.6 us -> 41.1 us (0.85)
  Pallas kernels: 45.4 us -> 38.8 us
  local copies, waits for them, and re-layouts: 3.05 us -> 1.32 us
  other arithmetic: 0 us -> 0.83 us
    pallas_call x1, Pallas kernels: 45.4 us -> 38.8 us  [shards(): pl.pallas_call(kernel, out_shape=jax.ShapeDtypeStruct((TOK, WIDTH), BF16)...]
    unnamed x1, local copies, waits for them, and re-layouts: 3.05 us -> 1.32 us
    concatenate x0 -> x1, other arithmetic: none -> 0.83 us  [shards(): small = jnp.concatenate([qs.T, ks.T, vs.T, taps], axis=0)]
where the time goes in v3:
time: 41.1 us; the launch traced here: 41 us
  Pallas kernels  38.8 us (94%)
  local copies, waits for them, and re-layouts  1.32 us (3%)
  other arithmetic  0.83 us (2%)
    pallas_call x1, Pallas kernels, shards(): pl.pallas_call(kernel, out_shape=jax.ShapeDtypeStruct((TOK, WIDTH), BF16)...  38.8 us
    unnamed x1, local copies, waits for them, and re-layouts  1.32 us
    concatenate x1, other arithmetic, shards(): small = jnp.concatenate([qs.T, ks.T, vs.T, taps], axis=0)  0.83 us

profile of v3, /device:TPU:1, one launch (start us, length us, event | category | flops | bytes accessed | tf_op | source)
XLA Modules:
  0.0 41.0 jit_solution(8461206838952102366)
XLA Ops:
  0.0 0.8 %select_maximum_fusion.small = f32[16,2048]{1,0:T(8,128)S(1)} fusion(f32[4,33]{1,0:T(4,128)} %param.13, f32[4,2048]{1,0:T(4,128)} %bitcast.3, f32[4,2048]{1,0:T(4,128)} %bitcast.4, f32[4,2048]{1,0:T(4,128)} %bitcast.5), kind=kLoop, calls=%fused_computation | loop fusion | flops 163840 | bytes 229904 | tf_op jit(solution)/shard_map/concatenate | solution.py:395
  0.8 38.8 %nystrom.1 = bf16[2048,512]{1,0:T(8,128)(2,1)S(1)} custom-call(bf16[2048,512]{1,0:T(8,128)(2,1)} %q_hbm.1, bf16[2048,512]{1,0:T(8,128)(2,1)} %k_hbm.1, bf16[2048,512]{1,0:T(8,128)(2,1)} %v_hbm.1, f32[16,2048]{1,0:T(8,128)S(1)} %select_maximum_fusion.small), custom_call_target="tpu_custom_call" | custom-call | tf_op jit(solution)/shard_map/nystrom/pallas_call | solution.py:396
  39.7 1.3 %copy.9 = bf16[2048,512]{1,0:T(8,128)(2,1)} copy(bf16[2048,512]{1,0:T(8,128)(2,1)S(1)} %nystrom.1) | data formatting | bytes 4194304

commit v4 on v3

--- a/solution.py
+++ b/solution.py
@@ -32,6 +32,7 @@
 SLICE = HEAD_DIM // OWN
 PACK = LANDMARKS + 128
 NEAR_EARLY = 4
+CONV_SPLIT = 8
 
 
 def dot(a, b):
@@ -50,7 +51,7 @@
     q_hbm, k_hbm, v_hbm, small, out,
     q_v, k_v, v_raw, v_pad, vt, sc_qk, sc_v, lm_all, qm, km, kmt,
     mid, tops, score, wt, rs_send, rs_recv, x_ref, near, conv, mp_all, toep,
-    q_sem, k_sem, v_sem, lm_s, lm_r, halo_s, halo_r, top_s, top_r, rs_s, rs_r, mp_s, mp_r,
+    q_sem, k_sem, v_sem, lm_s, lm_r, halo_s, halo_r, top_s, top_r, rs_s, rs_r, mp_s, mp_r, go_sem,
 ):
     me = lax.axis_index("seq")
     zme = lax.axis_index("head")
@@ -82,18 +83,20 @@
 
     barrier = pltpu.get_barrier_semaphore()
 
-    def greet_seq(r, _):
-        pl.semaphore_signal(barrier, inc=1, device_id=(partner(r), zme), device_id_type=MESH)
+    def greet(r, _):
+        target = ((yme + r // 4) % 4) * 8 + ((xme + r % 4) % 4) * 2
+        pl.semaphore_signal(barrier, inc=1, device_id=(target, zme), device_id_type=MESH)
         return 0
 
-    def greet_head(r, _):
-        pl.semaphore_signal(
-            barrier, inc=1, device_id=(me, (zme + r) % HEADN), device_id_type=MESH
-        )
-        return 0
-
-    lax.fori_loop(1, SEQN, greet_seq, 0)
-    lax.fori_loop(1, HEADN, greet_head, 0)
+    lax.fori_loop(1, CHIPS, greet, 0)
+
+    @pl.when(cme == 1)
+    def _():
+        pl.semaphore_signal(barrier, inc=1, device_id=(other, zme), device_id_type=MESH)
+        for r in range(1, HEADN):
+            pl.semaphore_signal(
+                barrier, inc=1, device_id=(me, (zme + r) % HEADN), device_id_type=MESH
+            )
 
     sc_qk[...] = small[0 : 2 * HEADS, :].T
     sc_v[...] = small[2 * HEADS : 4 * HEADS, :].T
@@ -121,7 +124,14 @@
         both = jnp.concatenate([marks[h], marks[HEADS + h]], axis=0)
         lm_all[cme, chip, :, cols(h)] = both.astype(BF16)
 
-    pl.semaphore_wait(barrier, SEQN - 1 + HEADN - 1)
+    @pl.when(cme == 0)
+    def _():
+        pl.semaphore_wait(barrier, SEQN - 1)
+        pl.semaphore_signal(go_sem, inc=1, device_id=(other, zme), device_id_type=MESH)
+
+    @pl.when(cme == 1)
+    def _():
+        pl.semaphore_wait(go_sem, 1)
 
     def group_copy(buf, at, sems, n, target):
         return pltpu.make_async_remote_copy(
@@ -186,10 +196,12 @@
         conv_block(b)
         return 0
 
-    lax.fori_loop(1, TOK // 128 - 1, conv_inner, 0, unroll=2)
+    lax.fori_loop(1, CONV_SPLIT, conv_inner, 0, unroll=True)
 
     lm_total.wait_recv()
     lm_out.start()
+
+    lax.fori_loop(CONV_SPLIT, TOK // 128 - 1, conv_inner, 0, unroll=True)
 
     lm_in.wait_recv()
 
@@ -212,9 +224,13 @@
         col_top = jnp.maximum(col_top, jnp.max(c, axis=1, keepdims=True))
         row_top = jnp.maximum(row_top, jnp.max(r, axis=0, keepdims=True))
     first_half = lax.broadcasted_iota(jnp.int32, (8, 128), 0) < 4
-    tops[zme] = jnp.where(
+    own_top = jnp.where(
         first_half, jnp.broadcast_to(col_top, (8, 128)), jnp.broadcast_to(row_top, (8, 128))
     )
+
+    @pl.when(cme == 1)
+    def _():
+        tops[zme] = own_top
 
     def top_copy(at, target):
         return pltpu.make_async_remote_copy(
@@ -226,9 +242,21 @@
             device_id_type=MESH,
         )
 
-    for r in range(1, HEADN):
-        top_copy(zme, (zme + r) % HEADN).start()
+    @pl.when(cme == 1)
+    def _():
+        pl.semaphore_wait(barrier, HEADN - 1)
+        for r in range(1, HEADN):
+            top_copy(zme, (zme + r) % HEADN).start()
+
     top_total = top_copy(pl.ds(0, HEADN - 1), zme)
+    top_over = pltpu.make_async_remote_copy(
+        src_ref=tops,
+        dst_ref=tops,
+        send_sem=top_s.at[1],
+        recv_sem=top_r.at[1],
+        device_id=(other, zme),
+        device_id_type=MESH,
+    )
 
     def rs_copy(block, slot, target):
         return pltpu.make_async_remote_copy(
@@ -309,7 +337,14 @@
 
     lax.fori_loop(0, NEAR_EARLY, near_softmax, 0)
 
-    top_total.wait_recv()
+    @pl.when(cme == 1)
+    def _():
+        top_total.wait_recv()
+        top_over.start()
+
+    @pl.when(cme == 0)
+    def _():
+        top_over.wait_recv()
 
     best = jnp.max(tops[...], axis=0)
     scale = 1.0 / (best[0:1, 0:1] * best[4:5, 0:1])
@@ -380,7 +415,11 @@
     up.wait_send()
     lm_total.wait_send()
     lm_out.wait_send()
-    top_total.wait_send()
+    @pl.when(cme == 1)
+    def _():
+        top_total.wait_send()
+        top_over.wait_send()
+
     rs_total.wait_send()
     mp_total.wait_send()
     mp_out.wait_send()
@@ -428,12 +467,13 @@
             dma((2,)),
             dma((2,)),
             dma((2,)),
+            dma((2,)),
+            dma((2,)),
             dma((1,)),
             dma((1,)),
-            dma((1,)),
-            dma((1,)),
-            dma((2,)),
-            dma((2,)),
+            dma((2,)),
+            dma((2,)),
+            pltpu.SemaphoreType.REGULAR,
         ],
         compiler_params=pltpu.CompilerParams(
             collective_id=0, has_side_effects=True, vmem_limit_bytes=50 * 1024 * 1024

time: 41.1 us -> 38.8 us (0.944)
  Pallas kernels: 38.8 us -> 36.5 us
    pallas_call x1, Pallas kernels: 38.8 us -> 36.5 us  [shards(): pl.pallas_call(kernel, out_shape=jax.ShapeDtypeStruct((TOK, WIDTH), BF16)...]
where the time goes in v4:
time: 38.8 us; the launch traced here: 38.7 us
  Pallas kernels  36.5 us (94%)
  local copies, waits for them, and re-layouts  1.32 us (3%)
  other arithmetic  0.83 us (2%)
    pallas_call x1, Pallas kernels, shards(): pl.pallas_call(kernel, out_shape=jax.ShapeDtypeStruct((TOK, WIDTH), BF16)...  36.5 us
    unnamed x1, local copies, waits for them, and re-layouts  1.32 us
    concatenate x1, other arithmetic, shards(): small = jnp.concatenate([qs.T, ks.T, vs.T, taps], axis=0)  0.83 us

profile of v4, /device:TPU:1, one launch (start us, length us, event | category | flops | bytes accessed | tf_op | source)
XLA Modules:
  0.0 38.7 jit_solution(15271627177819745078)
XLA Ops:
  0.0 0.8 %select_maximum_fusion.small = f32[16,2048]{1,0:T(8,128)S(1)} fusion(f32[4,33]{1,0:T(4,128)} %param.13, f32[4,2048]{1,0:T(4,128)} %bitcast.3, f32[4,2048]{1,0:T(4,128)} %bitcast.4, f32[4,2048]{1,0:T(4,128)} %bitcast.5), kind=kLoop, calls=%fused_computation | loop fusion | flops 163840 | bytes 229904 | tf_op jit(solution)/shard_map/concatenate | solution.py:434
  0.8 36.5 %nystrom.1 = bf16[2048,512]{1,0:T(8,128)(2,1)S(1)} custom-call(bf16[2048,512]{1,0:T(8,128)(2,1)} %q_hbm.1, bf16[2048,512]{1,0:T(8,128)(2,1)} %k_hbm.1, bf16[2048,512]{1,0:T(8,128)(2,1)} %v_hbm.1, f32[16,2048]{1,0:T(8,128)S(1)} %select_maximum_fusion.small), custom_call_target="tpu_custom_call" | custom-call | tf_op jit(solution)/shard_map/nystrom/pallas_call | solution.py:435
  37.4 1.3 %copy.9 = bf16[2048,512]{1,0:T(8,128)(2,1)} copy(bf16[2048,512]{1,0:T(8,128)(2,1)S(1)} %nystrom.1) | data formatting | bytes 4194304

commit v5 on v4

v5 whole, which is shorter than its diff:
```python
import functools
import math

import jax
import jax.numpy as jnp
from jax import lax
from jax.experimental import pallas as pl
from jax.experimental.pallas import tpu as pltpu
from jax.sharding import PartitionSpec as P

MESH = pl.DeviceIdType.MESH
F32 = jnp.float32
BF16 = jnp.bfloat16
HEAD_DIM = 128
LANDMARKS = 256
SWEEPS = 6
TAPS = 33
REACH = TAPS // 2
LOG2E = math.log2(math.e)
SCALE2 = HEAD_DIM**-0.5 * LOG2E
FACTOR = HEAD_DIM**-0.5

TOK = 2048
HEADS = 4
WIDTH = HEADS * HEAD_DIM
SEQN = 32
HEADN = 8
SEGS = 8
SEG = 256
CHIPS = SEQN // 2
OWN = 8
SLICE = HEAD_DIM // OWN
NEAR_EARLY = 4
KEYS_EARLY = 2


def dot(a, b):
    return jnp.dot(a, b, preferred_element_type=F32)


def dot_nt(a, b):
    return lax.dot_general(a, b, (((1,), (1,)), ((), ())), preferred_element_type=F32)


def cols(h):
    return slice(h * HEAD_DIM, (h + 1) * HEAD_DIM)


def kernel(
    q_hbm, k_hbm, v_hbm, small, out,
    q_v, k_v, v_raw, v_pad, vt, sc_qk, sc_v, lm_all, qm, kmt,
    mid, tops, score, wt, rs_send, rs_recv, fact_send, fact_recv, x_ref, near, conv, mp_all, toep,
    q_sem, k_sem, v_sem, lm_s, lm_r, halo_s, halo_r, top_s, top_r, rs_s, rs_r, mp_s, mp_r, go_sem,
):
    me = lax.axis_index("seq")
    zme = lax.axis_index("head")
    yme, xme, cme = me // 8, (me // 2) % 4, me % 2
    h_me = 2 * ((xme + yme) % 2) + cme
    j_me = (me // 2) // 2
    chip = me // 2
    other = me + 1 - 2 * cme

    def partner(r):
        return (
            ((yme + r // 8) % 4) * 8 + ((xme + (r // 2) % 4) % 4) * 2 + (cme + r % 2) % 2
        )

    def across(r):
        return ((yme + r // 4) % 4) * 8 + ((xme + r % 4) % 4) * 2 + cme

    def owner(h, j):
        y = j // 2
        return (4 * y + 2 * (j % 2) + (h // 2 + y) % 2) * 2 + h % 2

    def rows_copy(src, dst, sem, i):
        rows = pl.ds(i * SEG, SEG)
        return pltpu.make_async_copy(src.at[rows], dst.at[rows], sem.at[i])

    barrier = pltpu.get_barrier_semaphore()

    def greet(r, _):
        target = ((yme + r // 4) % 4) * 8 + ((xme + r % 4) % 4) * 2
        pl.semaphore_signal(barrier, inc=1, device_id=(target, zme), device_id_type=MESH)
        return 0

    lax.fori_loop(1, CHIPS, greet, 0)

    @pl.when(cme == 1)
    def _():
        pl.semaphore_signal(barrier, inc=1, device_id=(other, zme), device_id_type=MESH)

    for i in range(SEGS):
        rows_copy(q_hbm, q_v, q_sem, i).start()
    for i in range(SEGS):
        rows_copy(k_hbm, k_v, k_sem, i).start()
    for i in range(SEGS):
        rows_copy(v_hbm, v_raw, v_sem, i).start()

    sc_qk[...] = small[0 : 2 * HEADS, :].T
    sc_v[...] = small[2 * HEADS : 4 * HEADS, :].T

    seg_id = lax.broadcasted_iota(jnp.int32, (SEGS, HEAD_DIM), 0)

    no_marks = (jnp.zeros((SEGS, HEAD_DIM), F32),) * HEADS

    def scale_means(t, src, buf, sem, first, end, marks):
        def segment(i, marks):
            rows = pl.ds(pl.multiple_of(i * SEG, SEG), SEG)
            rows_copy(src, buf, sem, i).wait()
            following = []
            for h in range(HEADS):
                n = t * HEADS + h
                x = (buf[rows, cols(h)].astype(F32) * sc_qk[rows, n : n + 1]).astype(BF16)
                buf[rows, cols(h)] = x
                mean = jnp.sum(x.astype(F32), axis=0, keepdims=True) * (1.0 / SEG)
                following.append(jnp.where(seg_id == i, mean, marks[h]))
            return tuple(following)

        return lax.fori_loop(first, end, segment, marks)

    def own_marks(t, marks):
        for n in range(2):
            both = jnp.concatenate([marks[n], marks[n + 2]], axis=0)
            lm_all[t, cme, chip, :, cols(n)] = both.astype(BF16)

    own_marks(0, scale_means(0, q_hbm, q_v, q_sem, 0, SEGS, no_marks))
    key_marks = scale_means(1, k_hbm, k_v, k_sem, 0, KEYS_EARLY, no_marks)

    @pl.when(cme == 0)
    def _():
        pl.semaphore_wait(barrier, SEQN - 1)
        pl.semaphore_signal(go_sem, inc=1, device_id=(other, zme), device_id_type=MESH)

    @pl.when(cme == 1)
    def _():
        pl.semaphore_wait(go_sem, 1)
        for r in range(1, HEADN):
            pl.semaphore_signal(
                barrier, inc=1, device_id=(me, (zme + r) % HEADN), device_id_type=MESH
            )

    def group_copy(buf, at, sems, n, target):
        return pltpu.make_async_remote_copy(
            src_ref=buf.at[at],
            dst_ref=buf.at[at],
            send_sem=sems[0].at[n],
            recv_sem=sems[1].at[n],
            device_id=(target, zme),
            device_id_type=MESH,
        )

    def leave(t):
        for r in range(1, CHIPS):
            group_copy(lm_all, (t, cme, chip), (lm_s, lm_r), t, across(r)).start()

    lm_total = [
        group_copy(lm_all, (t, 0, pl.ds(0, CHIPS - 1)), (lm_s, lm_r), t, other) for t in range(2)
    ]
    lm_out = [group_copy(lm_all, (t, cme), (lm_s, lm_r), 2 + t, other) for t in range(2)]
    lm_in = [group_copy(lm_all, (t, 1 - cme), (lm_s, lm_r), 2 + t, other) for t in range(2)]
    leave(0)

    own_marks(1, scale_means(1, k_hbm, k_v, k_sem, KEYS_EARLY, SEGS, key_marks))
    leave(1)

    def scale_v(i, _):
        rows = pl.ds(pl.multiple_of(i * SEG, SEG), SEG)
        out_rows = pl.ds(pl.multiple_of(i * SEG + REACH, REACH), SEG)
        rows_copy(v_hbm, v_raw, v_sem, i).wait()
        for h in range(HEADS):
            x = (v_raw[rows, cols(h)].astype(F32) * sc_v[rows, h : h + 1]).astype(BF16)
            v_pad[out_rows, cols(h)] = x
            vt[h, :, rows] = x.astype(F32).T.astype(BF16)
        return 0

    lax.fori_loop(0, SEGS, scale_v, 0, unroll=2)
    v_pad[TOK + 2 * REACH :, :] = jnp.zeros((128 - 2 * REACH, WIDTH), BF16)

    after, before = (me + 1) % SEQN, (me + SEQN - 1) % SEQN
    down = pltpu.make_async_remote_copy(
        src_ref=v_pad.at[pl.ds(TOK, REACH)],
        dst_ref=v_pad.at[pl.ds(0, REACH)],
        send_sem=halo_s.at[0],
        recv_sem=halo_r.at[0],
        device_id=(after, zme),
        device_id_type=MESH,
    )
    up = pltpu.make_async_remote_copy(
        src_ref=v_pad.at[pl.ds(REACH, REACH)],
        dst_ref=v_pad.at[pl.ds(TOK + REACH, REACH)],
        send_sem=halo_s.at[1],
        recv_sem=halo_r.at[1],
        device_id=(before, zme),
        device_id_type=MESH,
    )
    down.start()
    up.start()

    for h in range(HEADS):
        line = jnp.broadcast_to(small[3 * HEADS + h : 3 * HEADS + h + 1, 0:256], (128, 256))
        toep[h] = pltpu.roll(line, 0, 1, stride=1, stride_axis=0).astype(BF16)

    def conv_block(b):
        window = pl.ds(pl.multiple_of(b * 128, 128), 256)
        rows = pl.ds(pl.multiple_of(b * 128, 128), 128)
        for h in range(HEADS):
            conv[rows, cols(h)] = dot(toep[h], v_pad[window, cols(h)])

    def conv_inner(b, _):
        conv_block(b)
        return 0

    lm_total[0].wait_recv()
    lm_out[0].start()

    lax.fori_loop(1, TOK // 128 - 1, conv_inner, 0, unroll=True)

    lm_total[1].wait_recv()
    lm_out[1].start()

    lm_in[0].wait_recv()

    def by_head(t, h):
        both = lm_all[t, :, :, :, cols(h % 2)].reshape(SEQN, 2 * SEGS, HEAD_DIM).astype(F32)
        at = (h // 2) * SEGS
        return both[:, at : at + SEGS].reshape(LANDMARKS, HEAD_DIM)

    for h in range(HEADS):
        qm[h] = by_head(0, h).astype(BF16)

    def rs_copy(bufs, n, block, slot, target):
        return pltpu.make_async_remote_copy(
            src_ref=bufs[0].at[block],
            dst_ref=bufs[1].at[slot],
            send_sem=rs_s.at[n],
            recv_sem=rs_r.at[n],
            device_id=(target, zme),
            device_id_type=MESH,
        )

    sums, facts = (rs_send, rs_recv), (fact_send, fact_recv)
    tops_of, totals_of = {}, {}

    def far_scores(h):
        def chunk(i, top):
            rows = pl.ds(pl.multiple_of(i * SEG, SEG), SEG)
            s = dot_nt(k_v[rows, cols(h)], qm[h])
            score[h % 2, rows, :] = s
            return jnp.maximum(top, jnp.max(s.reshape(SEG // 8, 8, LANDMARKS), axis=0))

        top = lax.fori_loop(
            0, SEGS, chunk, jnp.full((8, LANDMARKS), -jnp.inf, F32), unroll=True
        )
        tops_of[h] = jnp.max(top, axis=0, keepdims=True)

    def far_weights(h):
        top = tops_of[h]

        def chunk(i, total):
            rows = pl.ds(pl.multiple_of(i * SEG, SEG), SEG)
            e = jnp.exp2((score[h % 2, rows, :] - top) * SCALE2)
            wt[h % 2, rows, :] = e.astype(BF16)
            return total + jnp.sum(e.reshape(SEG // 8, 8, LANDMARKS), axis=0)

        total = lax.fori_loop(0, SEGS, chunk, jnp.zeros((8, LANDMARKS), F32), unroll=True)
        totals_of[h] = jnp.sum(total, axis=0, keepdims=True)

    def far_sums(h):
        summed = dot(vt[h], wt[h % 2])
        rs_send[h * OWN : (h + 1) * OWN] = summed.astype(BF16).reshape(OWN, SLICE, LANDMARKS)
        top, total = tops_of[h], totals_of[h]
        lines = jnp.concatenate(
            [top[:, :128], top[:, 128:], total[:, :128], total[:, 128:]], axis=0
        )
        fact_send[h * OWN : (h + 1) * OWN] = jnp.broadcast_to(lines[None], (OWN, 4, 128))

    def far_leave(h):
        for n in range(1, OWN):
            j = (n + j_me) % OWN
            target = owner(h, j)
            rs_copy(sums, 0, h * OWN + j, me, target).start()
            rs_copy(facts, 1, h * OWN + j, me, target).start()

    far_scores(0)
    far_scores(1)

    lm_in[1].wait_recv()
    for h in range(HEADS):
        kmt[h] = by_head(1, h).T.astype(BF16)

    col_top = jnp.zeros((1, 1), F32)
    row_top = jnp.zeros((1, 1), F32)
    for h in range(HEADS):
        s = dot(qm[h], kmt[h])
        e = jnp.exp2((s - jnp.max(s, axis=1, keepdims=True)) * SCALE2)
        m = e / jnp.sum(e, axis=1, keepdims=True)
        mid[h] = m
        c = jnp.sum(m, axis=0, keepdims=True)
        r = jnp.sum(m, axis=1, keepdims=True)
        col_top = jnp.maximum(col_top, jnp.max(c, axis=1, keepdims=True))
        row_top = jnp.maximum(row_top, jnp.max(r, axis=0, keepdims=True))
    first_half = lax.broadcasted_iota(jnp.int32, (8, 128), 0) < 4
    own_top = jnp.where(
        first_half, jnp.broadcast_to(col_top, (8, 128)), jnp.broadcast_to(row_top, (8, 128))
    )

    tops[zme] = own_top

    def top_copy(at, core, target):
        return pltpu.make_async_remote_copy(
            src_ref=tops.at[at],
            dst_ref=tops.at[at],
            send_sem=top_s.at[core],
            recv_sem=top_r.at[0],
            device_id=(2 * chip + core, target),
            device_id_type=MESH,
        )

    @pl.when(cme == 1)
    def _():
        pl.semaphore_wait(barrier, HEADN - 1)
        for r in range(1, HEADN):
            top_copy(zme, 0, (zme + r) % HEADN).start()
            top_copy(zme, 1, (zme + r) % HEADN).start()

    top_total = [top_copy(pl.ds(0, HEADN - 1), core, zme) for core in range(2)]

    far_weights(0)
    far_sums(0)
    far_scores(2)
    far_weights(1)
    far_leave(0)
    far_sums(1)
    far_scores(3)
    far_weights(2)
    far_leave(1)
    far_sums(2)
    far_weights(3)
    far_leave(2)
    far_sums(3)
    far_leave(3)
    for n in range(1, HEADS):
        h = (h_me + n) % HEADS
        rs_copy(sums, 0, h * OWN + j_me, me, owner(h, j_me)).start()
        rs_copy(facts, 1, h * OWN + j_me, me, owner(h, j_me)).start()
    rs_total = [
        rs_copy(bufs, n, pl.ds(0, SEQN - 1), pl.ds(0, SEQN - 1), other)
        for n, bufs in enumerate((sums, facts))
    ]
    rs_recv[me] = rs_send[h_me * OWN + j_me]
    fact_recv[me] = fact_send[h_me * OWN + j_me]

    down.wait_recv()
    up.wait_recv()
    v_pad[0:REACH, :] = jnp.where(me == 0, jnp.zeros((REACH, WIDTH), BF16), v_pad[0:REACH, :])
    v_pad[TOK + REACH : TOK + 2 * REACH, :] = jnp.where(
        me == SEQN - 1, jnp.zeros((REACH, WIDTH), BF16), v_pad[TOK + REACH : TOK + 2 * REACH, :]
    )
    conv_block(0)
    conv_block(TOK // 128 - 1)

    def near_softmax(i, _):
        rows = pl.ds(pl.multiple_of(i * SEG, SEG), SEG)
        for h in range(HEADS):
            s = dot(q_v[rows, cols(h)], kmt[h])
            e = jnp.exp2((s - jnp.max(s, axis=1, keepdims=True)) * SCALE2)
            near[h, rows, :] = (e * (1.0 / jnp.sum(e, axis=1, keepdims=True))).astype(BF16)
        return 0

    lax.fori_loop(0, NEAR_EARLY, near_softmax, 0)

    m = mid[h_me]
    mb = m.astype(BF16)
    x_ref[0:LANDMARKS, :] = dot(m.T.astype(BF16), mb)
    x_ref[LANDMARKS:, :] = m
    top_total[0].wait_recv()

    best = jnp.max(tops[...], axis=0)
    scale = 1.0 / (best[0:1, 0:1] * best[4:5, 0:1])
    x = x_ref[...] * scale
    for sweep in range(SWEEPS):
        xb = x.astype(BF16)
        y = dot(xb, xb[:LANDMARKS])
        b = (7.0 * x[:LANDMARKS] - y[:LANDMARKS]).astype(BF16)
        if sweep == SWEEPS - 1:
            x, y = x[LANDMARKS:], y[LANDMARKS:]
        x = 0.25 * (13.0 * x - 15.0 * y + dot(y.astype(BF16), b))
    iterated = x.astype(BF16)

    for copy in rs_total:
        copy.wait_recv()


    top = jnp.max(fact_recv[...], axis=0)

    def combine(s, carry):
        num, den = carry
        lines = fact_recv[s]
        e = jnp.exp2((lines - top) * SCALE2)
        w = jnp.concatenate([e[0:1], e[1:2]], axis=1)
        part = jnp.concatenate([lines[2:3], lines[3:4]], axis=1)
        return num + rs_recv[s].astype(F32) * w, den + part * w

    num, den = lax.fori_loop(
        0,
        SEQN,
        combine,
        (jnp.zeros((SLICE, LANDMARKS), F32), jnp.zeros((1, LANDMARKS), F32)),
        unroll=4,
    )
    reduced = (num / den).astype(BF16)
    slot = (h_me // 2) * OWN + j_me
    mp_all[cme, slot] = dot(reduced, iterated).astype(BF16)
    for r in range(1, CHIPS):
        group_copy(mp_all, (cme, slot), (mp_s, mp_r), 0, across(r)).start()
    mp_total = group_copy(mp_all, (0, pl.ds(0, CHIPS - 1)), (mp_s, mp_r), 0, other)
    mp_out = group_copy(mp_all, (cme,), (mp_s, mp_r), 1, other)
    mp_in = group_copy(mp_all, (1 - cme,), (mp_s, mp_r), 1, other)

    lax.fori_loop(NEAR_EARLY, SEGS, near_softmax, 0)

    mp_total.wait_recv()
    mp_out.start()

    def attend(h):
        lanes = pl.ds(pl.multiple_of(h * HEAD_DIM, HEAD_DIM), HEAD_DIM)
        mapped = mp_all[h % 2, pl.ds((h // 2) * OWN, OWN)].reshape(HEAD_DIM, LANDMARKS).astype(F32).T.astype(BF16)
        for i in range(4):
            rows = slice(i * 512, (i + 1) * 512)
            out[rows, lanes] = (dot(near[h, rows, :], mapped) + conv[rows, lanes]).astype(BF16)

    attend(cme)
    attend(cme + 2)

    mp_in.wait_recv()

    attend(1 - cme)
    attend(3 - cme)

    down.wait_send()
    up.wait_send()
    for copy in lm_total + lm_out:
        copy.wait_send()
    @pl.when(cme == 1)
    def _():
        for copy in top_total:
            copy.wait_send()

    for copy in rs_total:
        copy.wait_send()
    mp_total.wait_send()
    mp_out.wait_send()


def shards(q, k, v, qs, ks, vs, cw):
    dma = pltpu.SemaphoreType.DMA
    vm = pltpu.VMEM
    hbm = pl.BlockSpec(memory_space=pl.ANY)
    whole = pl.BlockSpec(memory_space=pltpu.VMEM)
    taps = jnp.pad(cw, ((0, 0), (0, TOK - TAPS)))
    small = jnp.concatenate([qs.T, ks.T, vs.T, taps], axis=0)
    return pl.pallas_call(
        kernel,
        out_shape=jax.ShapeDtypeStruct((TOK, WIDTH), BF16),
        in_specs=[hbm, hbm, hbm, whole],
        out_specs=whole,
        scratch_shapes=[
            vm((TOK, WIDTH), BF16),
            vm((TOK, WIDTH), BF16),
            vm((TOK, WIDTH), BF16),
            vm((TOK + 128, WIDTH), BF16),
            vm((HEADS, HEAD_DIM, TOK), BF16),
            vm((TOK, 8), F32),
            vm((TOK, 8), F32),
            vm((2, 2, CHIPS, 2 * SEGS, WIDTH // 2), BF16),
            vm((HEADS, LANDMARKS, HEAD_DIM), BF16),
            vm((HEADS, HEAD_DIM, LANDMARKS), BF16),
            vm((HEADS, LANDMARKS, LANDMARKS), F32),
            vm((HEADN, 8, 128), F32),
            vm((2, TOK, LANDMARKS), F32),
            vm((2, TOK, LANDMARKS), BF16),
            vm((SEQN, SLICE, LANDMARKS), BF16),
            vm((SEQN, SLICE, LANDMARKS), BF16),
            vm((SEQN, 4, 128), F32),
            vm((SEQN, 4, 128), F32),
            vm((2 * LANDMARKS, LANDMARKS), F32),
            vm((HEADS, TOK, LANDMARKS), BF16),
            vm((TOK, WIDTH), F32),
            vm((2, CHIPS, SLICE, LANDMARKS), BF16),
            vm((HEADS, 128, 256), BF16),
            dma((SEGS,)),
            dma((SEGS,)),
            dma((SEGS,)),
            dma((4,)),
            dma((4,)),
            dma((2,)),
            dma((2,)),
            dma((2,)),
            dma((2,)),
            dma((2,)),
            dma((2,)),
            dma((2,)),
            dma((2,)),
            pltpu.SemaphoreType.REGULAR,
        ],
        compiler_params=pltpu.CompilerParams(
            collective_id=0, has_side_effects=True, vmem_limit_bytes=50 * 1024 * 1024
        ),
        name="nystrom",
    )(q, k, v, small)


def solution(mesh):
    tokens, heads = P("seq", "head"), P("head", None)
    return jax.shard_map(
        shards, mesh=mesh, in_specs=(tokens,) * 6 + (heads,), out_specs=tokens, check_vma=False
    )
```

time: 38.8 us -> 37.2 us (0.959)
  Pallas kernels: 36.5 us -> 34.9 us
    pallas_call x1, Pallas kernels: 36.5 us -> 34.9 us  [shards(): pl.pallas_call(kernel, out_shape=jax.ShapeDtypeStruct((TOK, WIDTH), BF16)...]
where the time goes in v5:
time: 37.2 us; the launch traced here: 37.1 us
  Pallas kernels  34.9 us (94%)
  local copies, waits for them, and re-layouts  1.32 us (4%)
  other arithmetic  0.83 us (2%)
    pallas_call x1, Pallas kernels, shards(): pl.pallas_call(kernel, out_shape=jax.ShapeDtypeStruct((TOK, WIDTH), BF16)...  34.9 us
    unnamed x1, local copies, waits for them, and re-layouts  1.32 us
    concatenate x1, other arithmetic, shards(): small = jnp.concatenate([qs.T, ks.T, vs.T, taps], axis=0)  0.83 us

profile of v5, /device:TPU:1, one launch (start us, length us, event | category | flops | bytes accessed | tf_op | source)
XLA Modules:
  0.0 37.1 jit_solution(15572428795936536863)
XLA Ops:
  0.0 0.8 %select_maximum_fusion.small = f32[16,2048]{1,0:T(8,128)S(1)} fusion(f32[4,33]{1,0:T(4,128)} %param.13, f32[4,2048]{1,0:T(4,128)} %bitcast.3, f32[4,2048]{1,0:T(4,128)} %bitcast.4, f32[4,2048]{1,0:T(4,128)} %bitcast.5), kind=kLoop, calls=%fused_computation | loop fusion | flops 163840 | bytes 229904 | tf_op jit(solution)/shard_map/concatenate | solution.py:461
  0.8 34.9 %nystrom.1 = bf16[2048,512]{1,0:T(8,128)(2,1)S(1)} custom-call(bf16[2048,512]{1,0:T(8,128)(2,1)} %q_hbm.1, bf16[2048,512]{1,0:T(8,128)(2,1)} %k_hbm.1, bf16[2048,512]{1,0:T(8,128)(2,1)} %v_hbm.1, f32[16,2048]{1,0:T(8,128)S(1)} %select_maximum_fusion.small), custom_call_target="tpu_custom_call" | custom-call | tf_op jit(solution)/shard_map/nystrom/pallas_call | solution.py:462
  35.7 1.3 %copy.9 = bf16[2048,512]{1,0:T(8,128)(2,1)} copy(bf16[2048,512]{1,0:T(8,128)(2,1)S(1)} %nystrom.1) | data formatting | bytes 4194304

commit v6 on v5

--- a/solution.py
+++ b/solution.py
@@ -30,8 +30,7 @@
 CHIPS = SEQN // 2
 OWN = 8
 SLICE = HEAD_DIM // OWN
-NEAR_EARLY = 4
-KEYS_EARLY = 2
+KEYS_EARLY = 3
 
 
 def dot(a, b):
@@ -49,7 +48,7 @@
 def kernel(
     q_hbm, k_hbm, v_hbm, small, out,
     q_v, k_v, v_raw, v_pad, vt, sc_qk, sc_v, lm_all, qm, kmt,
-    mid, tops, score, wt, rs_send, rs_recv, fact_send, fact_recv, x_ref, near, conv, mp_all, toep,
+    mid, tops, score, wt, rs_send, rs_recv, fact_send, fact_recv, x_ref, near, conv, rd_all, mp_all, toep,
     q_sem, k_sem, v_sem, lm_s, lm_r, halo_s, halo_r, top_s, top_r, rs_s, rs_r, mp_s, mp_r, go_sem,
 ):
     me = lax.axis_index("seq")
@@ -76,19 +75,6 @@
         rows = pl.ds(i * SEG, SEG)
         return pltpu.make_async_copy(src.at[rows], dst.at[rows], sem.at[i])
 
-    barrier = pltpu.get_barrier_semaphore()
-
-    def greet(r, _):
-        target = ((yme + r // 4) % 4) * 8 + ((xme + r % 4) % 4) * 2
-        pl.semaphore_signal(barrier, inc=1, device_id=(target, zme), device_id_type=MESH)
-        return 0
-
-    lax.fori_loop(1, CHIPS, greet, 0)
-
-    @pl.when(cme == 1)
-    def _():
-        pl.semaphore_signal(barrier, inc=1, device_id=(other, zme), device_id_type=MESH)
-
     for i in range(SEGS):
         rows_copy(q_hbm, q_v, q_sem, i).start()
     for i in range(SEGS):
@@ -96,8 +82,17 @@
     for i in range(SEGS):
         rows_copy(v_hbm, v_raw, v_sem, i).start()
 
+    barrier = pltpu.get_barrier_semaphore()
+
+    for r in range(1, CHIPS):
+        target = ((yme + r // 4) % 4) * 8 + ((xme + r % 4) % 4) * 2
+        pl.semaphore_signal(barrier, inc=1, device_id=(target, zme), device_id_type=MESH)
+
+    @pl.when(cme == 1)
+    def _():
+        pl.semaphore_signal(barrier, inc=1, device_id=(other, zme), device_id_type=MESH)
+
     sc_qk[...] = small[0 : 2 * HEADS, :].T
-    sc_v[...] = small[2 * HEADS : 4 * HEADS, :].T
 
     seg_id = lax.broadcasted_iota(jnp.int32, (SEGS, HEAD_DIM), 0)
 
@@ -163,6 +158,7 @@
     own_marks(1, scale_means(1, k_hbm, k_v, k_sem, KEYS_EARLY, SEGS, key_marks))
     leave(1)
 
+    sc_v[...] = small[2 * HEADS : 4 * HEADS, :].T
     def scale_v(i, _):
         rows = pl.ds(pl.multiple_of(i * SEG, SEG), SEG)
         out_rows = pl.ds(pl.multiple_of(i * SEG + REACH, REACH), SEG)
@@ -367,29 +363,10 @@
             near[h, rows, :] = (e * (1.0 / jnp.sum(e, axis=1, keepdims=True))).astype(BF16)
         return 0
 
-    lax.fori_loop(0, NEAR_EARLY, near_softmax, 0)
-
-    m = mid[h_me]
-    mb = m.astype(BF16)
-    x_ref[0:LANDMARKS, :] = dot(m.T.astype(BF16), mb)
-    x_ref[LANDMARKS:, :] = m
-    top_total[0].wait_recv()
-
-    best = jnp.max(tops[...], axis=0)
-    scale = 1.0 / (best[0:1, 0:1] * best[4:5, 0:1])
-    x = x_ref[...] * scale
-    for sweep in range(SWEEPS):
-        xb = x.astype(BF16)
-        y = dot(xb, xb[:LANDMARKS])
-        b = (7.0 * x[:LANDMARKS] - y[:LANDMARKS]).astype(BF16)
-        if sweep == SWEEPS - 1:
-            x, y = x[LANDMARKS:], y[LANDMARKS:]
-        x = 0.25 * (13.0 * x - 15.0 * y + dot(y.astype(BF16), b))
-    iterated = x.astype(BF16)
+    lax.fori_loop(0, SEGS, near_softmax, 0)
 
     for copy in rs_total:
         copy.wait_recv()
-
 
     top = jnp.max(fact_recv[...], axis=0)
 
@@ -410,21 +387,43 @@
     )
     reduced = (num / den).astype(BF16)
     slot = (h_me // 2) * OWN + j_me
-    mp_all[cme, slot] = dot(reduced, iterated).astype(BF16)
+    rd_all[slot] = reduced
     for r in range(1, CHIPS):
-        group_copy(mp_all, (cme, slot), (mp_s, mp_r), 0, across(r)).start()
-    mp_total = group_copy(mp_all, (0, pl.ds(0, CHIPS - 1)), (mp_s, mp_r), 0, other)
+        group_copy(rd_all, (slot,), (mp_s, mp_r), 0, across(r)).start()
+    rd_total = group_copy(rd_all, (pl.ds(0, CHIPS - 1),), (mp_s, mp_r), 0, other)
     mp_out = group_copy(mp_all, (cme,), (mp_s, mp_r), 1, other)
     mp_in = group_copy(mp_all, (1 - cme,), (mp_s, mp_r), 1, other)
 
-    lax.fori_loop(NEAR_EARLY, SEGS, near_softmax, 0)
-
-    mp_total.wait_recv()
+    for n in range(2):
+        m = mid[cme + 2 * n]
+        x_ref[n, 0:LANDMARKS, :] = dot(m.T.astype(BF16), m.astype(BF16))
+        x_ref[n, LANDMARKS:, :] = m
+    top_total[0].wait_recv()
+
+    best = jnp.max(tops[...], axis=0)
+    scale = 1.0 / (best[0:1, 0:1] * best[4:5, 0:1])
+    xs = [x_ref[n] * scale for n in range(2)]
+    for sweep in range(SWEEPS):
+        for n in range(2):
+            x = xs[n]
+            xb = x.astype(BF16)
+            y = dot(xb, xb[:LANDMARKS])
+            b = (7.0 * x[:LANDMARKS] - y[:LANDMARKS]).astype(BF16)
+            if sweep == SWEEPS - 1:
+                x, y = x[LANDMARKS:], y[LANDMARKS:]
+            xs[n] = 0.25 * (13.0 * x - 15.0 * y + dot(y.astype(BF16), b))
+    iterated = [x.astype(BF16) for x in xs]
+
+    rd_total.wait_recv()
+
+    for n in range(2):
+        rows = rd_all[n * OWN : (n + 1) * OWN].reshape(HEAD_DIM, LANDMARKS)
+        mp_all[cme, n] = dot(rows, iterated[n]).astype(BF16)
     mp_out.start()
 
     def attend(h):
         lanes = pl.ds(pl.multiple_of(h * HEAD_DIM, HEAD_DIM), HEAD_DIM)
-        mapped = mp_all[h % 2, pl.ds((h // 2) * OWN, OWN)].reshape(HEAD_DIM, LANDMARKS).astype(F32).T.astype(BF16)
+        mapped = mp_all[h % 2, h // 2].astype(F32).T.astype(BF16)
         for i in range(4):
             rows = slice(i * 512, (i + 1) * 512)
             out[rows, lanes] = (dot(near[h, rows, :], mapped) + conv[rows, lanes]).astype(BF16)
@@ -448,7 +447,7 @@
 
     for copy in rs_total:
         copy.wait_send()
-    mp_total.wait_send()
+    rd_total.wait_send()
     mp_out.wait_send()
 
 
@@ -483,10 +482,11 @@
             vm((SEQN, SLICE, LANDMARKS), BF16),
             vm((SEQN, 4, 128), F32),
             vm((SEQN, 4, 128), F32),
-            vm((2 * LANDMARKS, LANDMARKS), F32),
+            vm((2, 2 * LANDMARKS, LANDMARKS), F32),
             vm((HEADS, TOK, LANDMARKS), BF16),
             vm((TOK, WIDTH), F32),
-            vm((2, CHIPS, SLICE, LANDMARKS), BF16),
+            vm((CHIPS, SLICE, LANDMARKS), BF16),
+            vm((2, 2, HEAD_DIM, LANDMARKS), BF16),
             vm((HEADS, 128, 256), BF16),
             dma((SEGS,)),
             dma((SEGS,)),

time: 37.2 us -> 34.3 us (0.922)
  Pallas kernels: 34.9 us -> 32 us
    pallas_call x1, Pallas kernels: 34.9 us -> 32 us  [shards(): pl.pallas_call(kernel, out_shape=jax.ShapeDtypeStruct((TOK, WIDTH), BF16)...]
where the time goes in v6:
time: 34.3 us; the launch traced here: 34.2 us
  Pallas kernels  32 us (93%)
  local copies, waits for them, and re-layouts  1.32 us (4%)
  other arithmetic  0.83 us (2%)
    pallas_call x1, Pallas kernels, shards(): pl.pallas_call(kernel, out_shape=jax.ShapeDtypeStruct((TOK, WIDTH), BF16)...  32 us
    unnamed x1, local copies, waits for them, and re-layouts  1.32 us
    concatenate x1, other arithmetic, shards(): small = jnp.concatenate([qs.T, ks.T, vs.T, taps], axis=0)  0.83 us

profile of v6, /device:TPU:1, one launch (start us, length us, event | category | flops | bytes accessed | tf_op | source)
XLA Modules:
  0.0 34.2 jit_solution(359992317960176651)
XLA Ops:
  0.0 0.8 %select_maximum_fusion.small = f32[16,2048]{1,0:T(8,128)S(1)} fusion(f32[4,33]{1,0:T(4,128)} %param.13, f32[4,2048]{1,0:T(4,128)} %bitcast.3, f32[4,2048]{1,0:T(4,128)} %bitcast.4, f32[4,2048]{1,0:T(4,128)} %bitcast.5), kind=kLoop, calls=%fused_computation | loop fusion | flops 163840 | bytes 229904 | tf_op jit(solution)/shard_map/concatenate | solution.py:460
  0.8 32.0 %nystrom.1 = bf16[2048,512]{1,0:T(8,128)(2,1)S(1)} custom-call(bf16[2048,512]{1,0:T(8,128)(2,1)} %q_hbm.1, bf16[2048,512]{1,0:T(8,128)(2,1)} %k_hbm.1, bf16[2048,512]{1,0:T(8,128)(2,1)} %v_hbm.1, f32[16,2048]{1,0:T(8,128)S(1)} %select_maximum_fusion.small), custom_call_target="tpu_custom_call" | custom-call | tf_op jit(solution)/shard_map/nystrom/pallas_call | solution.py:461
  32.9 1.3 %copy.9 = bf16[2048,512]{1,0:T(8,128)(2,1)} copy(bf16[2048,512]{1,0:T(8,128)(2,1)S(1)} %nystrom.1) | data formatting | bytes 4194304

commit v7 on v6

--- a/solution.py
+++ b/solution.py
@@ -262,13 +262,12 @@
         totals_of[h] = jnp.sum(total, axis=0, keepdims=True)
 
     def far_sums(h):
-        summed = dot(vt[h], wt[h % 2])
+        total = totals_of[h]
+        summed = dot(vt[h], wt[h % 2]) * (1.0 / total)
         rs_send[h * OWN : (h + 1) * OWN] = summed.astype(BF16).reshape(OWN, SLICE, LANDMARKS)
-        top, total = tops_of[h], totals_of[h]
-        lines = jnp.concatenate(
-            [top[:, :128], top[:, 128:], total[:, :128], total[:, 128:]], axis=0
-        )
-        fact_send[h * OWN : (h + 1) * OWN] = jnp.broadcast_to(lines[None], (OWN, 4, 128))
+        level = tops_of[h] * SCALE2 + jnp.log(total) * LOG2E
+        lines = jnp.concatenate([level[:, :128], level[:, 128:]], axis=0)
+        fact_send[h * OWN : (h + 1) * OWN] = jnp.broadcast_to(lines[None], (OWN, 2, 128))
 
     def far_leave(h):
         for n in range(1, OWN):
@@ -279,6 +278,9 @@
 
     far_scores(0)
     far_scores(1)
+    far_weights(0)
+    far_sums(0)
+    far_leave(0)
 
     lm_in[1].wait_recv()
     for h in range(HEADS):
@@ -321,15 +323,12 @@
 
     top_total = [top_copy(pl.ds(0, HEADN - 1), core, zme) for core in range(2)]
 
-    far_weights(0)
-    far_sums(0)
     far_scores(2)
     far_weights(1)
-    far_leave(0)
     far_sums(1)
     far_scores(3)
+    far_leave(1)
     far_weights(2)
-    far_leave(1)
     far_sums(2)
     far_weights(3)
     far_leave(2)
@@ -372,11 +371,9 @@
 
     def combine(s, carry):
         num, den = carry
-        lines = fact_recv[s]
-        e = jnp.exp2((lines - top) * SCALE2)
+        e = jnp.exp2(fact_recv[s] - top)
         w = jnp.concatenate([e[0:1], e[1:2]], axis=1)
-        part = jnp.concatenate([lines[2:3], lines[3:4]], axis=1)
-        return num + rs_recv[s].astype(F32) * w, den + part * w
+        return num + rs_recv[s].astype(F32) * w, den + w
 
     num, den = lax.fori_loop(
         0,
@@ -480,8 +477,8 @@
             vm((2, TOK, LANDMARKS), BF16),
             vm((SEQN, SLICE, LANDMARKS), BF16),
             vm((SEQN, SLICE, LANDMARKS), BF16),
-            vm((SEQN, 4, 128), F32),
-            vm((SEQN, 4, 128), F32),
+            vm((SEQN, 2, 128), F32),
+            vm((SEQN, 2, 128), F32),
             vm((2, 2 * LANDMARKS, LANDMARKS), F32),
             vm((HEADS, TOK, LANDMARKS), BF16),
             vm((TOK, WIDTH), F32),

time: 34.3 us -> 34.1 us (level)
  no operation moved by 1% of the time
where the time goes in v7:
time: 34.1 us; the launch traced here: 34 us
  Pallas kernels  31.8 us (93%)
  local copies, waits for them, and re-layouts  1.32 us (4%)
  other arithmetic  0.83 us (2%)
    pallas_call x1, Pallas kernels, shards(): pl.pallas_call(kernel, out_shape=jax.ShapeDtypeStruct((TOK, WIDTH), BF16)...  31.8 us
    unnamed x1, local copies, waits for them, and re-layouts  1.32 us
    concatenate x1, other arithmetic, shards(): small = jnp.concatenate([qs.T, ks.T, vs.T, taps], axis=0)  0.83 us

profile of v7, /device:TPU:1, one launch (start us, length us, event | category | flops | bytes accessed | tf_op | source)
XLA Modules:
  0.0 34.0 jit_solution(5082088485805199549)
XLA Ops:
  0.0 0.8 %select_maximum_fusion.small = f32[16,2048]{1,0:T(8,128)S(1)} fusion(f32[4,33]{1,0:T(4,128)} %param.13, f32[4,2048]{1,0:T(4,128)} %bitcast.3, f32[4,2048]{1,0:T(4,128)} %bitcast.4, f32[4,2048]{1,0:T(4,128)} %bitcast.5), kind=kLoop, calls=%fused_computation | loop fusion | flops 163840 | bytes 229904 | tf_op jit(solution)/shard_map/concatenate | solution.py:457
  0.8 31.8 %nystrom.1 = bf16[2048,512]{1,0:T(8,128)(2,1)S(1)} custom-call(bf16[2048,512]{1,0:T(8,128)(2,1)} %q_hbm.1, bf16[2048,512]{1,0:T(8,128)(2,1)} %k_hbm.1, bf16[2048,512]{1,0:T(8,128)(2,1)} %v_hbm.1, f32[16,2048]{1,0:T(8,128)S(1)} %select_maximum_fusion.small), custom_call_target="tpu_custom_call" | custom-call | tf_op jit(solution)/shard_map/nystrom/pallas_call | solution.py:458
  32.7 1.3 %copy.9 = bf16[2048,512]{1,0:T(8,128)(2,1)} copy(bf16[2048,512]{1,0:T(8,128)(2,1)S(1)} %nystrom.1) | data formatting | bytes 4194304

commit v8 on v7

--- a/solution.py
+++ b/solution.py
@@ -31,6 +31,13 @@
 OWN = 8
 SLICE = HEAD_DIM // OWN
 KEYS_EARLY = 3
+
+
+def hops(r):
+    return min(r // 4, 4 - r // 4) + min(r % 4, 4 - r % 4)
+
+
+FAR_FIRST = sorted(range(1, CHIPS), key=hops, reverse=True)
 
 
 def dot(a, b):
@@ -84,7 +91,7 @@
 
     barrier = pltpu.get_barrier_semaphore()
 
-    for r in range(1, CHIPS):
+    for r in FAR_FIRST:
         target = ((yme + r // 4) % 4) * 8 + ((xme + r % 4) % 4) * 2
         pl.semaphore_signal(barrier, inc=1, device_id=(target, zme), device_id_type=MESH)
 
@@ -145,7 +152,7 @@
         )
 
     def leave(t):
-        for r in range(1, CHIPS):
+        for r in FAR_FIRST:
             group_copy(lm_all, (t, cme, chip), (lm_s, lm_r), t, across(r)).start()
 
     lm_total = [
@@ -385,7 +392,7 @@
     reduced = (num / den).astype(BF16)
     slot = (h_me // 2) * OWN + j_me
     rd_all[slot] = reduced
-    for r in range(1, CHIPS):
+    for r in FAR_FIRST:
         group_copy(rd_all, (slot,), (mp_s, mp_r), 0, across(r)).start()
     rd_total = group_copy(rd_all, (pl.ds(0, CHIPS - 1),), (mp_s, mp_r), 0, other)
     mp_out = group_copy(mp_all, (cme,), (mp_s, mp_r), 1, other)

time: 34.1 us -> 33.6 us (0.985)
  Pallas kernels: 31.8 us -> 31.3 us
    pallas_call x1, Pallas kernels: 31.8 us -> 31.3 us  [shards(): pl.pallas_call(kernel, out_shape=jax.ShapeDtypeStruct((TOK, WIDTH), BF16)...]
where the time goes in v8:
time: 33.6 us; the launch traced here: 33.5 us
  Pallas kernels  31.3 us (93%)
  local copies, waits for them, and re-layouts  1.32 us (4%)
  other arithmetic  0.83 us (2%)
    pallas_call x1, Pallas kernels, shards(): pl.pallas_call(kernel, out_shape=jax.ShapeDtypeStruct((TOK, WIDTH), BF16)...  31.3 us
    unnamed x1, local copies, waits for them, and re-layouts  1.32 us
    concatenate x1, other arithmetic, shards(): small = jnp.concatenate([qs.T, ks.T, vs.T, taps], axis=0)  0.83 us

profile of v8, /device:TPU:1, one launch (start us, length us, event | category | flops | bytes accessed | tf_op | source)
XLA Modules:
  0.0 33.5 jit_solution(15978914875143603208)
XLA Ops:
  0.0 0.8 %select_maximum_fusion.small = f32[16,2048]{1,0:T(8,128)S(1)} fusion(f32[4,33]{1,0:T(4,128)} %param.13, f32[4,2048]{1,0:T(4,128)} %bitcast.3, f32[4,2048]{1,0:T(4,128)} %bitcast.4, f32[4,2048]{1,0:T(4,128)} %bitcast.5), kind=kLoop, calls=%fused_computation | loop fusion | flops 163840 | bytes 229904 | tf_op jit(solution)/shard_map/concatenate | solution.py:464
  0.8 31.3 %nystrom.1 = bf16[2048,512]{1,0:T(8,128)(2,1)S(1)} custom-call(bf16[2048,512]{1,0:T(8,128)(2,1)} %q_hbm.1, bf16[2048,512]{1,0:T(8,128)(2,1)} %k_hbm.1, bf16[2048,512]{1,0:T(8,128)(2,1)} %v_hbm.1, f32[16,2048]{1,0:T(8,128)S(1)} %select_maximum_fusion.small), custom_call_target="tpu_custom_call" | custom-call | tf_op jit(solution)/shard_map/nystrom/pallas_call | solution.py:465
  32.1 1.3 %copy.9 = bf16[2048,512]{1,0:T(8,128)(2,1)} copy(bf16[2048,512]{1,0:T(8,128)(2,1)S(1)} %nystrom.1) | data formatting | bytes 4194304
